TPU v7x, 128 devices: a whole 4x4x4 slice. The times are simulated.
128 devices in a mesh: dom: 8 (over y, z_lo), grp: 16 (over z_hi, x, core).
Axes of the slice: x: 4, y: 4, z: 4 (z_hi: 2, z_lo: 2; z = z_hi * 2 + z_lo), core: 2. Of those that a mesh axis runs over, the one named last changes fastest.
Arguments:
- states: float32 [262144, 128], P(('dom', 'grp')), may hold values from -6 to 6
- potential: float32 [262144], P(('dom', 'grp')), may hold values from 0.3 to 3
- cell_scale: float32 [32768], P(('dom', 'grp')), may hold values from 0.25 to 1
- stiffness: float32 [27, 27], replicated
- connect: int32 [27, 32768], P(None, ('dom', 'grp')), may hold values from 0 to 2559, as said below
- face_nodes: int32 [2, 32768], P(None, ('dom', 'grp')), may hold values from 0 to 2047, as said below
- node_count: int32 [128], P(('dom', 'grp')), may hold values from 512 to 2048, as said below
- filter_cut: float32 [1], replicated, may hold values from 8 to 20
- spectrum_top: float32 [1], replicated, may hold values from 100 to 160
Outputs:
- ortho_states: float32 [262144, 128], P(('dom', 'grp'))
- projected: float32 [512, 32], P('grp')
Inputs may be any that keep to these rules, and one draw needn't show every extreme that they name: `connect`: cell k of a domain lies in cell block b = k // 32 and references only rows of the extended list that are lower ghosts (0 .. 255), upper ghosts (2304 and above), or owned slots s (row 256 + s) with min(b, 6) * 256 <= s < min(b, 6) * 256 + 2 * 256; owned slots referenced by live cells are below the domain's node count. `face_nodes`: indices of live node slots of the domain; within one domain the lower and the upper lists each hold distinct nodes. `node_count`: A multiple of 32; some domain has exactly 2048.
All inputs are finite; a program needn't handle non-finite values.
Results may differ from a plain program's by a relative error of at most 0.0003.
Values sent between devices are 32-bit elements; how exact they have to be, the bound alone decides.
A program may use at most 128 MiB of HBM per device.

v0:
```python
import jax
import jax.numpy as jnp
from jax import lax
from jax.sharding import PartitionSpec as P

NB = 8
DEG = 4


HIGH = lax.Precision.HIGHEST


def extended(block, sides, width):
    for axis, dim in sides:
        count = lax.axis_size(axis)
        forward = [(i, i + 1) for i in range(count - 1)]
        backward = [(target, source) for source, target in forward]
        low = lax.ppermute(
            lax.slice_in_dim(block, block.shape[dim] - width, None, axis=dim), axis, forward
        )
        high = lax.ppermute(lax.slice_in_dim(block, 0, width, axis=dim), axis, backward)
        block = jnp.concatenate([low, block, high], axis=dim)
    return block


def block_term(index, total, ext, connect, scale, stiffness, face):
    per_block = face // 8
    width = ext.shape[1]
    start = jnp.minimum(index, 6) * face
    part_conn = lax.dynamic_slice_in_dim(connect, index * per_block, per_block, 1)
    part_scale = lax.dynamic_slice_in_dim(scale, index * per_block, per_block, 0)
    column = jnp.where(
        part_conn < face,
        part_conn,
        jnp.where(part_conn >= 9 * face, part_conn - 6 * face, part_conn - start),
    )
    onehot = (column.reshape(-1)[:, None] == jnp.arange(4 * face, dtype=jnp.int32)[None, :]).astype(
        jnp.float32
    )
    window = lax.dynamic_slice_in_dim(ext, face + start, 2 * face, 0)
    sub = jnp.concatenate([ext[:face], window, ext[9 * face :]], axis=0)
    gathered = jnp.dot(onehot, sub, precision=HIGH).reshape(part_conn.shape[0], per_block, width)
    local = (
        jnp.einsum("ab,bcv->acv", stiffness, gathered, precision=HIGH) * part_scale[None, :, None]
    )
    contrib = jnp.dot(onehot.T, local.reshape(-1, width), precision=HIGH)
    owned = lax.dynamic_slice_in_dim(total, face + start, 2 * face, 0) + contrib[face : 3 * face]
    total = lax.dynamic_update_slice_in_dim(total, owned, face + start, 0)
    total = total.at[:face].add(contrib[:face])
    total = total.at[9 * face :].add(contrib[3 * face :])
    return total


def hamil(field, potential, scale, stiffness, connect, low_pick, high_pick):
    face = low_pick.shape[0]
    count = field.shape[0]
    lows = jnp.dot(low_pick, field, precision=HIGH)
    highs = jnp.dot(high_pick, field, precision=HIGH)
    padded = extended(jnp.concatenate([lows, highs], axis=0), ((("dom", "grp"), 0),), face)
    ext = jnp.concatenate([padded[:face], field, padded[3 * face :]], axis=0)
    empty = jnp.zeros(ext.shape, jnp.float32)
    per_block = face // 8
    blocks_all = connect.shape[1] // per_block
    out = empty
    for index in range(blocks_all):
        out = block_term(index, out, ext, connect, scale, stiffness, face)
    own = out[face : face + count] + potential[:, None] * field
    returned = extended(
        jnp.concatenate([out[:face], out[face + count :]], axis=0), ((("dom", "grp"), 0),), face
    )
    own = own + jnp.dot(low_pick.T, returned[:face], precision=HIGH)
    own = own + jnp.dot(high_pick.T, returned[3 * face :], precision=HIGH)
    return own


def arrange(full, rows_grid, cols_grid, block):
    size = full.shape[0]
    tiles = full.reshape(
        size // (rows_grid * block), rows_grid, block, size // (cols_grid * block), cols_grid, block
    )
    tiles = tiles.transpose(1, 4, 0, 2, 3, 5)
    return tiles.reshape(rows_grid * cols_grid, size // rows_grid, size // cols_grid)


def body(
    states,
    potential,
    cell_scale,
    stiffness,
    connect,
    face_nodes,
    node_count,
    filter_cut,
    spectrum_top,
):
    count = states.shape[0]
    width = states.shape[1]
    live_nodes = node_count[0]
    live_cells = live_nodes // 8
    node_mask = (jnp.arange(count, dtype=jnp.int32) < live_nodes).astype(jnp.float32)
    cell_mask = (jnp.arange(cell_scale.shape[0], dtype=jnp.int32) < live_cells).astype(jnp.float32)
    scale = cell_scale * cell_mask
    positions = jnp.arange(count, dtype=jnp.int32)[None, :]
    low_pick = (face_nodes[0][:, None] == positions).astype(jnp.float32)
    high_pick = (face_nodes[1][:, None] == positions).astype(jnp.float32)

    def apply_h(field):
        return hamil(field, potential, scale, stiffness, connect, low_pick, high_pick)

    half = (spectrum_top[0] - filter_cut[0]) * 0.5
    centre = (spectrum_top[0] + filter_cut[0]) * 0.5
    previous = states * node_mask[:, None]
    current = (apply_h(previous) - centre * previous) / half
    for step in range(DEG - 1):
        following = 2.0 * (apply_h(current) - centre * current) / half - previous
        previous, current = (current, following)
    hfiltered = apply_h(current)
    total_nodes = lax.axis_size("dom") * lax.axis_size("grp") * count
    correlation_part = jnp.dot(current.T, current, precision=HIGH) / total_nodes
    identity = jnp.eye(width, dtype=jnp.float32)
    rows_grid = lax.axis_size("grp") // 4
    hgram_part = jnp.dot(current.T, hfiltered, precision=HIGH) / total_nodes
    correlation, hgram = lax.psum((correlation_part, hgram_part), ("dom", "grp"))
    factor = jnp.linalg.cholesky(correlation)
    inverse = jax.scipy.linalg.solve_triangular(factor, identity, lower=True)
    ortho_states = jnp.dot(current, inverse.T, precision=HIGH)
    hhat = jnp.dot(jnp.dot(inverse, hgram, precision=HIGH), inverse.T, precision=HIGH)
    pieces = arrange(hhat, rows_grid, 4, NB)
    projected = lax.dynamic_index_in_dim(pieces, lax.axis_index("grp"), 0, keepdims=False)
    return (ortho_states, projected)


def solution(mesh):
    placed = (
        P(("dom", "grp"), None),
        P(("dom", "grp")),
        P(("dom", "grp")),
        P(),
        P(None, ("dom", "grp")),
        P(None, ("dom", "grp")),
        P(("dom", "grp")),
        P(),
        P(),
    )
    return jax.shard_map(
        body,
        mesh=mesh,
        in_specs=placed,
        out_specs=(P(("dom", "grp"), None), P("grp", None)),
        check_vma=False,
    )
```

profile of v0, /device:TPU:1, one launch (start us, length us, event | category | flops | bytes accessed | tf_op | source)
XLA Modules:
  0.0 608.1 jit_solution(3024688675078295067)
XLA Ops:
  11.4 3.3 collective-permute-start.1
  16.0 3.6 collective-permute-start
  31.8 3.4 fusion.78
  46.3 3.4 fusion.58
  60.7 3.6 fusion.38
  75.4 3.3 fusion.18
  82.2 4.5 collective-permute-start.2
  95.2 4.6 collective-permute-start.4
  149.1 3.5 fusion.16
  154.8 4.4 collective-permute-start.6
  168.5 3.7 collective-permute-start.8
  221.4 3.5 fusion.14
  227.1 4.4 collective-permute-start.10
  240.8 3.7 collective-permute-start.12
  268.4 3.2 fusion.52
  274.9 3.2 fusion.42
  294.1 3.5 fusion.12
  299.8 4.4 collective-permute-start.14
  313.4 4.3 collective-permute-start.16
  367.0 3.4 fusion.10
  375.0 7.2 %collective-permute-start.18 = (f32[256,128]{1,0:T(8,128)S(1)}, f32[256,128]{1,0:T(8,128)S(1)}, u32[]{:S(2)}, u32[]{:S(2)}) collective-permute-start(f32[256,128]{1,0:T(8,128)S(1)} %get-tuple-element.964), channel_id=1, source_target_pairs={{0,1},{1,2},{2,3},{3,4},{4,5},{5,6},{6,7},{7,8},{8,9},{9,10},{10,1... | collective-permute-start | bytes 393224 | tf_op jit(solution)/shard_map/ppermute | solution.py:18
  388.8 181.9 %all-reduce.8.cloned.1.call-done = (f32[128,128]{0,1:T(8,128)}, f32[128,128]{0,1:T(8,128)}) async-done(((f32[128,128]{0,1:T(8,128)}, f32[128,128]{0,1:T(8,128)}), (f32[128,128]{0,1:T(8,128)}, f32[128,128]{0,1:T(8,128)})) %all-reduce.8.cloned.1.call-update) | async-done | bytes 131088 | tf_op jit(solution)/shard_map/psum | solution.py:123
  572.5 11.7 %cholesky.17 = f32[128,128]{1,0:T(8,128)S(1)} custom-call(f32[128,128]{1,0:T(8,128)S(1)} %fusion.427), custom_call_target="Cholesky" | custom-call | tf_op jit(solution)/shard_map/jit(cholesky)/cholesky | solution.py:124
  585.6 9.8 %custom-call.7 = f32[1,128,128]{1,2,0:T(8,128)S(1)} custom-call(f32[1,128,128]{2,1,0:T(8,128)S(1)} %fusion.424), custom_call_target="InvertDiagBlocksLowerTriangular" | custom-call | tf_op jit(solution)/shard_map/jit(_solve_triangular)/triangular_solve | solution.py:125
  (365 shorter events, 304.2 us)
Async XLA Ops:
  7.2 16.5 %copy-start = (f32[27,27]{1,0:T(8,128)S(1)}, f32[27,27]{1,0:T(8,128)}, u32[]{:S(2)}) copy-start(f32[27,27]{1,0:T(8,128)} %param.172) | copy-start | bytes 8752
  7.2 563.5 %all-reduce.8.cloned.1.call-start = ((), (), s32[]{:S(2)}) async-start(), calls=%async_computation | async-start | bytes 262144 | tf_op jit(solution)/shard_map/psum | solution.py:123
  11.4 9.2 %collective-permute-start.1 = (f32[256,128]{1,0:T(8,128)S(1)}, f32[256,128]{1,0:T(8,128)S(1)}, u32[]{:S(2)}, u32[]{:S(2)}) collective-permute-start(f32[256,128]{1,0:T(8,128)S(1)} %fusion.103), channel_id=1, source_target_pairs={{1,0},{2,1},{3,2},{4,3},{5,4},{6,5},{7,6},{8,7},{9,8},{10,9},{11,1... | collective-permute-start | bytes 393224 | tf_op jit(solution)/shard_map/ppermute | solution.py:21
  16.0 5.0 collective-permute-start
  78.9 9.7 %copy-start.3 = (f32[2048]{0:T(1024)S(1)}, f32[2048]{0:T(1024)}, u32[]{:S(2)}) copy-start(f32[2048]{0:T(1024)} %param.170) | copy-start | bytes 24580
  79.0 7.7 %collective-permute-start.3 = (f32[256,128]{1,0:T(8,128)S(1)}, f32[256,128]{1,0:T(8,128)S(1)}, u32[]{:S(2)}, u32[]{:S(2)}) collective-permute-start(f32[256,128]{1,0:T(8,128)S(1)} %get-tuple-element.973), channel_id=1, source_target_pairs={{1,0},{2,1},{3,2},{4,3},{5,4},{6,5},{7,6},{8,7},{9,8},{10,9},{11,1... | collective-permute-start | bytes 393224 | tf_op jit(solution)/shard_map/ppermute | solution.py:21
  82.2 6.4 %collective-permute-start.2 = (f32[256,128]{1,0:T(8,128)S(1)}, f32[256,128]{1,0:T(8,128)S(1)}, u32[]{:S(2)}, u32[]{:S(2)}) collective-permute-start(f32[256,128]{1,0:T(8,128)S(1)} %get-tuple-element.972), channel_id=1, source_target_pairs={{0,1},{1,2},{2,3},{3,4},{4,5},{5,6},{6,7},{7,8},{8,9},{9,10},{10,1... | collective-permute-start | bytes 393224 | tf_op jit(solution)/shard_map/ppermute | solution.py:18
  93.3 7.0 %collective-permute-start.5 = (f32[256,128]{1,0:T(8,128)S(1)}, f32[256,128]{1,0:T(8,128)S(1)}, u32[]{:S(2)}, u32[]{:S(2)}) collective-permute-start(f32[256,128]{1,0:T(8,128)S(1)} %fusion.102), channel_id=1, source_target_pairs={{1,0},{2,1},{3,2},{4,3},{5,4},{6,5},{7,6},{8,7},{9,8},{10,9},{11,1... | collective-permute-start | bytes 393224 | tf_op jit(solution)/shard_map/ppermute | solution.py:21
  95.2 6.3 %collective-permute-start.4 = (f32[256,128]{1,0:T(8,128)S(1)}, f32[256,128]{1,0:T(8,128)S(1)}, u32[]{:S(2)}, u32[]{:S(2)}) collective-permute-start(f32[256,128]{1,0:T(8,128)S(1)} %fusion.111), channel_id=1, source_target_pairs={{0,1},{1,2},{2,3},{3,4},{4,5},{5,6},{6,7},{7,8},{8,9},{9,10},{10,1... | collective-permute-start | bytes 393224 | tf_op jit(solution)/shard_map/ppermute | solution.py:18
  152.9 7.0 %collective-permute-start.7 = (f32[256,128]{1,0:T(8,128)S(1)}, f32[256,128]{1,0:T(8,128)S(1)}, u32[]{:S(2)}, u32[]{:S(2)}) collective-permute-start(f32[256,128]{1,0:T(8,128)S(1)} %get-tuple-element.971), channel_id=1, source_target_pairs={{1,0},{2,1},{3,2},{4,3},{5,4},{6,5},{7,6},{8,7},{9,8},{10,9},{11,1... | collective-permute-start | bytes 393224 | tf_op jit(solution)/shard_map/ppermute | solution.py:21
  154.8 7.0 %collective-permute-start.6 = (f32[256,128]{1,0:T(8,128)S(1)}, f32[256,128]{1,0:T(8,128)S(1)}, u32[]{:S(2)}, u32[]{:S(2)}) collective-permute-start(f32[256,128]{1,0:T(8,128)S(1)} %get-tuple-element.970), channel_id=1, source_target_pairs={{0,1},{1,2},{2,3},{3,4},{4,5},{5,6},{6,7},{7,8},{8,9},{9,10},{10,1... | collective-permute-start | bytes 393224 | tf_op jit(solution)/shard_map/ppermute | solution.py:18
  166.6 6.3 %collective-permute-start.9 = (f32[256,128]{1,0:T(8,128)S(1)}, f32[256,128]{1,0:T(8,128)S(1)}, u32[]{:S(2)}, u32[]{:S(2)}) collective-permute-start(f32[256,128]{1,0:T(8,128)S(1)} %fusion.101), channel_id=1, source_target_pairs={{1,0},{2,1},{3,2},{4,3},{5,4},{6,5},{7,6},{8,7},{9,8},{10,9},{11,1... | collective-permute-start | bytes 393224 | tf_op jit(solution)/shard_map/ppermute | solution.py:21
  168.5 5.6 collective-permute-start.8
  225.2 7.0 %collective-permute-start.11 = (f32[256,128]{1,0:T(8,128)S(1)}, f32[256,128]{1,0:T(8,128)S(1)}, u32[]{:S(2)}, u32[]{:S(2)}) collective-permute-start(f32[256,128]{1,0:T(8,128)S(1)} %get-tuple-element.969), channel_id=1, source_target_pairs={{1,0},{2,1},{3,2},{4,3},{5,4},{6,5},{7,6},{8,7},{9,8},{10,9},{11,1... | collective-permute-start | bytes 393224 | tf_op jit(solution)/shard_map/ppermute | solution.py:21
  227.1 7.0 %collective-permute-start.10 = (f32[256,128]{1,0:T(8,128)S(1)}, f32[256,128]{1,0:T(8,128)S(1)}, u32[]{:S(2)}, u32[]{:S(2)}) collective-permute-start(f32[256,128]{1,0:T(8,128)S(1)} %get-tuple-element.968), channel_id=1, source_target_pairs={{0,1},{1,2},{2,3},{3,4},{4,5},{5,6},{6,7},{7,8},{8,9},{9,10},{10,1... | collective-permute-start | bytes 393224 | tf_op jit(solution)/shard_map/ppermute | solution.py:18
  238.9 6.3 %collective-permute-start.13 = (f32[256,128]{1,0:T(8,128)S(1)}, f32[256,128]{1,0:T(8,128)S(1)}, u32[]{:S(2)}, u32[]{:S(2)}) collective-permute-start(f32[256,128]{1,0:T(8,128)S(1)} %fusion.100), channel_id=1, source_target_pairs={{1,0},{2,1},{3,2},{4,3},{5,4},{6,5},{7,6},{8,7},{9,8},{10,9},{11,1... | collective-permute-start | bytes 393224 | tf_op jit(solution)/shard_map/ppermute | solution.py:21
  240.8 5.6 collective-permute-start.12
  297.8 7.0 %collective-permute-start.15 = (f32[256,128]{1,0:T(8,128)S(1)}, f32[256,128]{1,0:T(8,128)S(1)}, u32[]{:S(2)}, u32[]{:S(2)}) collective-permute-start(f32[256,128]{1,0:T(8,128)S(1)} %get-tuple-element.967), channel_id=1, source_target_pairs={{1,0},{2,1},{3,2},{4,3},{5,4},{6,5},{7,6},{8,7},{9,8},{10,9},{11,1... | collective-permute-start | bytes 393224 | tf_op jit(solution)/shard_map/ppermute | solution.py:21
  299.8 7.0 %collective-permute-start.14 = (f32[256,128]{1,0:T(8,128)S(1)}, f32[256,128]{1,0:T(8,128)S(1)}, u32[]{:S(2)}, u32[]{:S(2)}) collective-permute-start(f32[256,128]{1,0:T(8,128)S(1)} %get-tuple-element.966), channel_id=1, source_target_pairs={{0,1},{1,2},{2,3},{3,4},{4,5},{5,6},{6,7},{7,8},{8,9},{9,10},{10,1... | collective-permute-start | bytes 393224 | tf_op jit(solution)/shard_map/ppermute | solution.py:18
  311.5 7.0 %collective-permute-start.17 = (f32[256,128]{1,0:T(8,128)S(1)}, f32[256,128]{1,0:T(8,128)S(1)}, u32[]{:S(2)}, u32[]{:S(2)}) collective-permute-start(f32[256,128]{1,0:T(8,128)S(1)} %fusion.99), channel_id=1, source_target_pairs={{1,0},{2,1},{3,2},{4,3},{5,4},{6,5},{7,6},{8,7},{9,8},{10,9},{11,1... | collective-permute-start | bytes 393224 | tf_op jit(solution)/shard_map/ppermute | solution.py:21
  313.4 6.2 %collective-permute-start.16 = (f32[256,128]{1,0:T(8,128)S(1)}, f32[256,128]{1,0:T(8,128)S(1)}, u32[]{:S(2)}, u32[]{:S(2)}) collective-permute-start(f32[256,128]{1,0:T(8,128)S(1)} %fusion.105), channel_id=1, source_target_pairs={{0,1},{1,2},{2,3},{3,4},{4,5},{5,6},{6,7},{7,8},{8,9},{9,10},{10,1... | collective-permute-start | bytes 393224 | tf_op jit(solution)/shard_map/ppermute | solution.py:18
  370.6 11.5 %collective-permute-start.19 = (f32[256,128]{1,0:T(8,128)S(1)}, f32[256,128]{1,0:T(8,128)S(1)}, u32[]{:S(2)}, u32[]{:S(2)}) collective-permute-start(f32[256,128]{1,0:T(8,128)S(1)} %get-tuple-element.965), channel_id=1, source_target_pairs={{1,0},{2,1},{3,2},{4,3},{5,4},{6,5},{7,6},{8,7},{9,8},{10,9},{11,1... | collective-permute-start | bytes 393224 | tf_op jit(solution)/shard_map/ppermute | solution.py:21
  375.0 9.1 %collective-permute-start.18 = (f32[256,128]{1,0:T(8,128)S(1)}, f32[256,128]{1,0:T(8,128)S(1)}, u32[]{:S(2)}, u32[]{:S(2)}) collective-permute-start(f32[256,128]{1,0:T(8,128)S(1)} %get-tuple-element.964), channel_id=1, source_target_pairs={{0,1},{1,2},{2,3},{3,4},{4,5},{5,6},{6,7},{7,8},{8,9},{9,10},{10,1... | collective-permute-start | bytes 393224 | tf_op jit(solution)/shard_map/ppermute | solution.py:18
  571.6 26.2 %copy-start.2 = (f32[128,128]{0,1:T(8,128)S(1)}, f32[128,128]{0,1:T(8,128)}, u32[]{:S(2)}) copy-start(f32[128,128]{0,1:T(8,128)} %get-tuple-element.963) | copy-start | bytes 196612
  (2 other events, 8.4 us)
Sparse Core Ops, SparseCore 0:
  388.9 181.7 all-reduce.7
where the time goes:
time: 612 us; the launch traced here: 608 us
  matrix products  283 us (46%)
  waiting for transfers between devices  191 us (31%)
  starting transfers between devices  65.2 us (11%)
  other arithmetic  31.7 us (5%)
  between operations  18.6 us (3%)
  local copies, waits for them, and re-layouts  18.5 us (3%)
    psum x1, waiting for transfers between devices, body(): lax.psum((correlation_part, hgram_part), ('dom', 'grp'))  182 us
    dot_general x40, matrix products, block_term(): contrib = jnp.dot(onehot.T, local.reshape(-1, width), precision=HIGH)  130 us
    dot_general x40, matrix products, block_term(): jnp.dot(onehot, sub, precision=HIGH)  76.3 us
    ppermute x10, starting transfers between devices, extended(): lax.ppermute(lax.slice_in_dim(block, block.shape[dim] - width, None, axis...  44.5 us
    dot_general x40, matrix products, block_term(): jnp.einsum('ab,bcv->acv', stiffness, gathered, precision=HIGH)  35.5 us
    ppermute x10, starting transfers between devices, extended(): lax.ppermute(lax.slice_in_dim(block, 0, width, axis=dim), axis, backward)  20.6 us
    another operation x3, other arithmetic, body(): factor = jnp.linalg.cholesky(correlation)  12.4 us
  transfers between devices with their start and end apart: 21, of which 13 were waited for; matrix products, arithmetic and copies ran while one was open for 2% of the time, Pallas kernels for 0%

commit v1 on v0

v1 whole, which is shorter than its diff:
```python
import functools

import jax
import jax.numpy as jnp
from jax import lax
from jax.experimental import pallas as pl
from jax.experimental.pallas import tpu as pltpu
from jax.sharding import PartitionSpec as P

NB = 8
NS = 128
NPC = 27
SLOTS = 28
DEG = 4
COUNT = 2048
FACE = 256
BLOCKS = 8
GROUPS = 4
GROWS = SLOTS * 8
ROWS = GROUPS * GROWS
WIN = 2 * FACE
GHOST = 2 * FACE

F32 = jnp.float32
BF16 = jnp.bfloat16
MESH = pl.DeviceIdType.MESH


def dot(a, b, dims=((1,), (0,))):
    return lax.dot_general(a, b, (dims, ((), ())), preferred_element_type=F32)


def split(x):
    hi = x.astype(BF16)
    lo = (x - hi.astype(F32)).astype(BF16)
    return jnp.concatenate([hi, lo], axis=1)


def halves(x):
    return x[:, :NS] + x[:, NS:]


def quarters(x):
    return (x[:NS, :NS] + x[NS:, NS:]) + (x[:NS, NS:] + x[NS:, :NS])


def filter_kernel(
    n_dom,
    n_grp,
    cut_ref,
    top_ref,
    live_ref,
    states_ref,
    pot_ref,
    scale_ref,
    kmat_ref,
    connr_ref,
    connc_ref,
    facer_ref,
    facec_ref,
    f_ref,
    corr_ref,
    hgram_ref,
    g_own,
    g_gho,
    t_own,
    t_gho,
    pick,
    pick_t,
    kk_hi,
    kk_lo,
    gath,
    loc,
    ext,
    extg,
    prev,
    work,
    face_send,
    face_recv,
    back_send,
    back_recv,
    ar_src,
    ar_slots,
    ar_part,
    ar_doms,
    ar_out,
    face_sems,
    back_sems,
    ar_sems1,
    ar_sems2,
    ar_sems3,
):
    dom = lax.axis_index("dom")
    grp = lax.axis_index("grp")
    total = n_dom * n_grp
    me = dom * n_grp + grp
    up = lax.rem(me + 1, total)
    down = lax.rem(me + total - 1, total)
    up_id = (up // n_grp, lax.rem(up, n_grp))
    down_id = (down // n_grp, lax.rem(down, n_grp))
    partners = [up_id, down_id]
    partners += [(dom, lax.rem(grp + s, n_grp)) for s in range(1, n_grp)]
    partners += [(lax.rem(dom + s, n_dom), grp) for s in range(1, n_dom)]
    barrier = pltpu.get_barrier_semaphore()
    for device in partners:
        pl.semaphore_signal(barrier, inc=1, device_id=device, device_id_type=MESH)

    def build(b, carry):
        lane8 = lax.broadcasted_iota(jnp.int32, (ROWS, BLOCKS), 1)
        col = jnp.sum(jnp.where(lane8 == b, connc_ref[...], 0), axis=1, keepdims=True)
        lane = lax.broadcasted_iota(jnp.int32, (ROWS, WIN), 1)
        g_own[b] = jnp.where(col == lane, 1.0, 0.0).astype(BF16)
        g_gho[b] = jnp.where(col == lane + WIN, 1.0, 0.0).astype(BF16)
        row = connr_ref[b]
        sub = lax.broadcasted_iota(jnp.int32, (WIN, ROWS), 0)
        t_own[b] = jnp.where(row == sub, 1.0, 0.0).astype(BF16)
        t_gho[:, pl.ds(pl.multiple_of(b * ROWS, 128), ROWS)] = jnp.where(
            row == sub + WIN, 1.0, 0.0
        ).astype(BF16)
        return carry

    lax.fori_loop(0, BLOCKS, build, 0)
    pick[...] = jnp.where(
        facec_ref[...] == lax.broadcasted_iota(jnp.int32, (2 * FACE, COUNT), 1), 1.0, 0.0
    ).astype(BF16)
    pick_t[...] = jnp.where(
        facer_ref[...] == lax.broadcasted_iota(jnp.int32, (COUNT, 2 * FACE), 0), 1.0, 0.0
    ).astype(BF16)
    spread = (
        lax.broadcasted_iota(jnp.int32, (GROWS, SLOTS), 0) // 8
        == lax.broadcasted_iota(jnp.int32, (GROWS, SLOTS), 1)
    )
    spread = jnp.where(spread, 1.0, 0.0).astype(F32)
    wide = lax.dot_general(
        spread, kmat_ref[...], (((1,), (0,)), ((), ())),
        precision=lax.Precision.HIGHEST, preferred_element_type=F32,
    )
    wide = lax.dot_general(
        wide, spread, (((1,), (1,)), ((), ())),
        precision=lax.Precision.HIGHEST, preferred_element_type=F32,
    )
    same = lax.rem(lax.broadcasted_iota(jnp.int32, (GROWS, GROWS), 0), 8) == lax.rem(
        lax.broadcasted_iota(jnp.int32, (GROWS, GROWS), 1), 8
    )
    wide = jnp.where(same, wide, 0.0)
    kk_hi[...] = wide.astype(BF16)
    kk_lo[...] = (wide - wide.astype(BF16).astype(F32)).astype(BF16)

    live = live_ref[0]
    rows = lax.broadcasted_iota(jnp.int32, (COUNT, NS), 0)
    f_ref[...] = jnp.where(rows < live, states_ref[...], 0.0)
    prev[...] = jnp.zeros((COUNT, NS), F32)
    half = (top_ref[0] - cut_ref[0]) * 0.5
    centre = (top_ref[0] + cut_ref[0]) * 0.5

    pl.semaphore_wait(barrier, len(partners))

    def exchange(send, recv, sems):
        down_copy = pltpu.make_async_remote_copy(
            src_ref=send.at[0], dst_ref=recv.at[1],
            send_sem=sems.at[0], recv_sem=sems.at[1],
            device_id=down_id, device_id_type=MESH,
        )
        up_copy = pltpu.make_async_remote_copy(
            src_ref=send.at[1], dst_ref=recv.at[0],
            send_sem=sems.at[2], recv_sem=sems.at[3],
            device_id=up_id, device_id_type=MESH,
        )
        down_copy.start()
        up_copy.start()
        return down_copy, up_copy

    def window(b):
        return pl.ds(pl.multiple_of(jnp.minimum(b, 6) * FACE, FACE), WIN)

    def load_field():
        def body(i, carry):
            at = pl.ds(pl.multiple_of(i * FACE, FACE), FACE)
            ext[at] = split(f_ref[at])
            return carry

        lax.fori_loop(0, COUNT // FACE, body, 0)

    def cells():
        load_field()
        sel = halves(dot(pick[...], ext[...]))
        face_send[0] = sel[:FACE]
        face_send[1] = sel[FACE:]
        copies = exchange(face_send, face_recv, face_sems)

        def owned(b, carry):
            gath[b] = dot(g_own[b], ext[window(b)]).astype(BF16)
            return carry

        lax.fori_loop(0, BLOCKS, owned, 0)
        for copy in copies:
            copy.wait()
        extg[0:FACE] = split(jnp.where(me == 0, 0.0, face_recv[0]))
        extg[FACE:] = split(jnp.where(me == total - 1, 0.0, face_recv[1]))

        def ghosts(b, carry):
            g = gath[b] + dot(g_gho[b], extg[...]).astype(BF16)
            for i in range(0, GROUPS, 2):
                one = g[i * GROWS : (i + 1) * GROWS]
                two = g[(i + 1) * GROWS : (i + 2) * GROWS]
                low = dot(kk_lo[...], jnp.concatenate([one[:, :NS], two[:, :NS]], axis=1))
                for j, part in enumerate((one, two)):
                    out = halves(dot(kk_hi[...], part)) + low[:, j * NS : (j + 1) * NS]
                    at = pl.ds(pl.multiple_of((b * GROUPS + i + j) * 8, 8), 8)
                    out = (out.reshape(SLOTS, 8, NS) * scale_ref[at][None]).reshape(GROWS, NS)
                    at = pl.ds(pl.multiple_of((b * GROUPS + i + j) * GROWS, 16), GROWS)
                    loc[at] = split(out)
            return carry

        lax.fori_loop(0, BLOCKS, ghosts, 0)

    def scatter_owned():
        work[...] = jnp.zeros((COUNT, NS), F32)

        def body(b, carry):
            at = pl.ds(pl.multiple_of(b * ROWS, 128), ROWS)
            work[window(b)] += halves(dot(t_own[b], loc[at]))
            return carry

        lax.fori_loop(0, BLOCKS, body, 0)

    def step(k, carry):
        alpha = jnp.where(k == 0, 1.0, 2.0) / half
        beta = jnp.where(k == 0, 0.0, 1.0)
        cells()
        back = halves(dot(t_gho[...], loc[...]))
        back_send[0] = back[:FACE]
        back_send[1] = back[FACE:]
        copies = exchange(back_send, back_recv, back_sems)
        scatter_owned()
        for copy in copies:
            copy.wait()
        extg[0:FACE] = split(jnp.where(me == 0, 0.0, back_recv[0]))
        extg[FACE:] = split(jnp.where(me == total - 1, 0.0, back_recv[1]))

        def body(i, carry):
            at = pl.ds(pl.multiple_of(i * FACE, FACE), FACE)
            added = work[at] + halves(dot(pick_t[at], extg[...]))
            cur = f_ref[at]
            new = alpha * (added + (pot_ref[at] - centre) * cur) - beta * prev[at]
            prev[at] = cur
            f_ref[at] = new
            return carry

        lax.fori_loop(0, COUNT // FACE, body, 0)
        return carry

    lax.fori_loop(0, DEG, step, 0)
    cells()
    corr = quarters(dot(ext[...], ext[...], ((0,), (0,))))
    scatter_owned()
    back = halves(dot(t_gho[...], loc[...]))
    hgram = quarters(dot(extg[...], split(back), ((0,), (0,))))

    def body(i, acc):
        at = pl.ds(pl.multiple_of(i * FACE, FACE), FACE)
        hf = work[at] + pot_ref[at] * f_ref[at]
        return acc + dot(ext[at], split(hf), ((0,), (0,)))

    acc = lax.fori_loop(0, COUNT // FACE, body, jnp.zeros((2 * NS, 2 * NS), F32))
    hgram = hgram + quarters(acc)

    inv_total = 1.0 / (total * COUNT)
    piece = NS // n_grp
    for j in range(n_grp):
        ar_src[j, :piece] = corr[j * piece : (j + 1) * piece] * inv_total
        ar_src[j, piece:] = hgram[j * piece : (j + 1) * piece] * inv_total
    copies = []
    for s in range(1, n_grp):
        other = lax.rem(grp + s, n_grp)
        copies.append(
            pltpu.make_async_remote_copy(
                src_ref=ar_src.at[other], dst_ref=ar_slots.at[s],
                send_sem=ar_sems1.at[0, s], recv_sem=ar_sems1.at[1, s],
                device_id=(dom, other), device_id_type=MESH,
            )
        )
    for copy in copies:
        copy.start()
    ar_slots[0] = ar_src[grp]
    for copy in copies:
        copy.wait()
    ar_part[...] = jnp.sum(ar_slots[...], axis=0)
    copies = []
    for s in range(1, n_dom):
        copies.append(
            pltpu.make_async_remote_copy(
                src_ref=ar_part, dst_ref=ar_doms.at[dom],
                send_sem=ar_sems2.at[0, s], recv_sem=ar_sems2.at[1, s],
                device_id=(lax.rem(dom + s, n_dom), grp), device_id_type=MESH,
            )
        )
    for copy in copies:
        copy.start()
    ar_doms[dom] = ar_part[...]
    for copy in copies:
        copy.wait()
    ar_part[...] = jnp.sum(ar_doms[...], axis=0)
    copies = []
    for s in range(1, n_grp):
        copies.append(
            pltpu.make_async_remote_copy(
                src_ref=ar_part, dst_ref=ar_out.at[grp],
                send_sem=ar_sems3.at[0, s], recv_sem=ar_sems3.at[1, s],
                device_id=(dom, lax.rem(grp + s, n_grp)), device_id_type=MESH,
            )
        )
    for copy in copies:
        copy.start()
    ar_out[grp] = ar_part[...]
    for copy in copies:
        copy.wait()
    for j in range(n_grp):
        corr_ref[j * piece : (j + 1) * piece] = ar_out[j, :piece]
        hgram_ref[j * piece : (j + 1) * piece] = ar_out[j, piece:]


def filtered_and_grams(n_dom, n_grp, operands):
    piece = NS // n_grp
    vmem = pl.BlockSpec(memory_space=pltpu.VMEM)
    smem = pl.BlockSpec(memory_space=pltpu.SMEM)
    dma = pltpu.SemaphoreType.DMA
    return pl.pallas_call(
        functools.partial(filter_kernel, n_dom, n_grp),
        out_shape=(
            jax.ShapeDtypeStruct((COUNT, NS), F32),
            jax.ShapeDtypeStruct((NS, NS), F32),
            jax.ShapeDtypeStruct((NS, NS), F32),
        ),
        in_specs=[smem] * 3 + [vmem] * 8,
        out_specs=(vmem, vmem, vmem),
        scratch_shapes=[
            pltpu.VMEM((BLOCKS, ROWS, WIN), BF16),
            pltpu.VMEM((BLOCKS, ROWS, GHOST), BF16),
            pltpu.VMEM((BLOCKS, WIN, ROWS), BF16),
            pltpu.VMEM((GHOST, BLOCKS * ROWS), BF16),
            pltpu.VMEM((2 * FACE, COUNT), BF16),
            pltpu.VMEM((COUNT, 2 * FACE), BF16),
            pltpu.VMEM((GROWS, GROWS), BF16),
            pltpu.VMEM((GROWS, GROWS), BF16),
            pltpu.VMEM((BLOCKS, ROWS, 2 * NS), BF16),
            pltpu.VMEM((BLOCKS * ROWS, 2 * NS), BF16),
            pltpu.VMEM((COUNT, 2 * NS), BF16),
            pltpu.VMEM((GHOST, 2 * NS), BF16),
            pltpu.VMEM((COUNT, NS), F32),
            pltpu.VMEM((COUNT, NS), F32),
            pltpu.VMEM((2, FACE, NS), F32),
            pltpu.VMEM((2, FACE, NS), F32),
            pltpu.VMEM((2, FACE, NS), F32),
            pltpu.VMEM((2, FACE, NS), F32),
            pltpu.VMEM((n_grp, 2 * piece, NS), F32),
            pltpu.VMEM((n_grp, 2 * piece, NS), F32),
            pltpu.VMEM((2 * piece, NS), F32),
            pltpu.VMEM((n_dom, 2 * piece, NS), F32),
            pltpu.VMEM((n_grp, 2 * piece, NS), F32),
            dma((4,)),
            dma((4,)),
            dma((2, n_grp)),
            dma((2, n_dom)),
            dma((2, n_grp)),
        ],
        compiler_params=pltpu.CompilerParams(
            collective_id=0, has_side_effects=True, vmem_limit_bytes=62 * 1024 * 1024
        ),
    )(*operands)


def finish_kernel(rows_grid, f_ref, corr_ref, hgram_ref, ortho_ref, tile_ref, inv_ref):
    grp = lax.axis_index("grp")
    sub = lax.broadcasted_iota(jnp.int32, (8, NS), 0)
    lane = lax.broadcasted_iota(jnp.int32, (8, NS), 1)
    panels = NS // 8
    high = lax.Precision.HIGHEST
    left = [corr_ref[8 * p : 8 * p + 8] for p in range(panels)]
    right = [jnp.where(lane == sub + 8 * p, 1.0, 0.0).astype(F32) for p in range(panels)]
    for p in range(panels):
        a, m = left[p], right[p]
        for j in range(8):
            c = 8 * p + j
            scale = 1.0 / jnp.sqrt(a[j : j + 1, c : c + 1])
            col = a[:, c : c + 1] * scale
            arow = a[j : j + 1] * scale
            mrow = m[j : j + 1] * scale
            a = jnp.where(sub > j, a - col * arow, jnp.where(sub == j, arow, a))
            m = jnp.where(sub > j, m - col * mrow, jnp.where(sub == j, mrow, m))
        inv_ref[8 * p : 8 * p + 8] = m
        if p + 1 < panels:
            both = lax.dot_general(
                a, jnp.concatenate([a, m], axis=1), (((0,), (0,)), ((), ())),
                precision=high, preferred_element_type=F32,
            )
            for q in range(p + 1, panels):
                left[q] = left[q] - both[8 * q : 8 * q + 8, :NS]
                right[q] = right[q] - both[8 * q : 8 * q + 8, NS:]
    inv = inv_ref[...]
    hi = inv.astype(BF16)
    lo = (inv - hi.astype(F32)).astype(BF16)
    wide = jnp.concatenate([hi, hi], axis=1)
    narrow = jnp.concatenate([lo, jnp.zeros_like(lo)], axis=1)
    weights = jnp.concatenate([wide, narrow], axis=0)

    def body(i, carry):
        at = pl.ds(pl.multiple_of(i * 256, 256), 256)
        ortho_ref[at] = halves(dot(split(f_ref[at]), weights, ((1,), (1,))))
        return carry

    lax.fori_loop(0, f_ref.shape[0] // 256, body, 0)
    r = grp // 4
    q = lax.rem(grp, 4)
    step = 8 * rows_grid
    mine = jnp.concatenate(
        [inv_ref[pl.ds(pl.multiple_of(step * t + 8 * r, 8), 8)] for t in range(NS // step)], axis=0
    )
    other = jnp.concatenate(
        [inv_ref[pl.ds(pl.multiple_of(32 * t + 8 * q, 8), 8)] for t in range(NS // 32)], axis=0
    )
    mine = jnp.dot(mine, hgram_ref[...], precision=high, preferred_element_type=F32)
    tile_ref[...] = lax.dot_general(
        mine, other, (((1,), (1,)), ((), ())), precision=high, preferred_element_type=F32
    )


def body(
    states,
    potential,
    cell_scale,
    stiffness,
    connect,
    face_nodes,
    node_count,
    filter_cut,
    spectrum_top,
):
    n_dom = lax.axis_size("dom")
    n_grp = lax.axis_size("grp")
    cells = cell_scale.shape[0]
    live_cells = node_count[0] // 8
    scale = jnp.where(jnp.arange(cells, dtype=jnp.int32) < live_cells, cell_scale, 0.0)
    scale = jnp.broadcast_to(scale[:, None], (cells, NS))
    pot = jnp.broadcast_to(potential[:, None], (COUNT, NS))
    start = jnp.minimum(jnp.arange(cells, dtype=jnp.int32) // 32, 6) * FACE
    column = jnp.where(
        connect < FACE,
        connect + WIN,
        jnp.where(connect >= FACE + COUNT, connect - FACE - COUNT + WIN + FACE, connect - FACE - start),
    )
    column = jnp.pad(column, ((0, SLOTS - NPC), (0, 0)), constant_values=-1)
    column = column.reshape(SLOTS, BLOCKS, GROUPS, 8).transpose(1, 2, 0, 3).reshape(BLOCKS, ROWS)
    kmat = jnp.pad(stiffness, ((0, SLOTS - NPC), (0, SLOTS - NPC)))
    f, corr, hgram = filtered_and_grams(
        n_dom,
        n_grp,
        (
            filter_cut,
            spectrum_top,
            node_count,
            states,
            pot,
            scale,
            kmat,
            column[:, None, :],
            column.T,
            face_nodes.reshape(1, -1),
            face_nodes.reshape(-1, 1),
        ),
    )
    rows_grid = n_grp // 4
    vmem = pl.BlockSpec(memory_space=pltpu.VMEM)
    return pl.pallas_call(
        functools.partial(finish_kernel, rows_grid),
        out_shape=(
            jax.ShapeDtypeStruct((COUNT, NS), F32),
            jax.ShapeDtypeStruct((NS // rows_grid, NS // 4), F32),
        ),
        in_specs=[vmem] * 3,
        out_specs=(vmem, vmem),
        scratch_shapes=[pltpu.VMEM((NS, NS), F32)],
        compiler_params=pltpu.CompilerParams(vmem_limit_bytes=32 * 1024 * 1024),
    )(f, corr, hgram)


def solution(mesh):
    placed = (
        P(("dom", "grp"), None),
        P(("dom", "grp")),
        P(("dom", "grp")),
        P(),
        P(None, ("dom", "grp")),
        P(None, ("dom", "grp")),
        P(("dom", "grp")),
        P(),
        P(),
    )
    return jax.shard_map(
        body,
        mesh=mesh,
        in_specs=placed,
        out_specs=(P(("dom", "grp"), None), P("grp", None)),
        check_vma=False,
    )
```

time: 612 us -> 187 us (0.31)
  matrix products: 283 us -> 0 us
  waiting for transfers between devices: 191 us -> 0 us
  Pallas kernels: 0 us -> 174 us
  starting transfers between devices: 65.2 us -> 0 us
  other arithmetic: 31.7 us -> 0.11 us
  between operations: 18.6 us -> 2.66 us
  local copies, waits for them, and re-layouts: 18.5 us -> 10.1 us
    dot_general x145 -> x0, matrix products: 283 us -> none  [the longest x40 130 us: block_term(): contrib = jnp.dot(onehot.T, local.reshape(-1, width), precision=HIGH)]
    psum x1 -> x0, waiting for transfers between devices: 182 us -> none  [body(): lax.psum((correlation_part, hgram_part), ('dom', 'grp'))]
    pallas_call x0 -> x2, Pallas kernels: none -> 174 us  [the longest x1 155 us: filtered_and_grams(): pl.pallas_call(functools.partial(filter_kernel, n_dom, n_grp), out_shape=...]
    ppermute x20 -> x0, starting transfers between devices: 65.1 us -> none  [the longest x10 44.5 us: extended(): lax.ppermute(lax.slice_in_dim(block, block.shape[dim] - width, None, axis...]
    another operation x5 -> x0, other arithmetic: 22.9 us -> none  [the longest x3 12.4 us: body(): factor = jnp.linalg.cholesky(correlation)]
    mul x40 -> x0, local copies, waits for them, and re-layouts: 10.5 us -> none  [block_term(): jnp.einsum('ab,bcv->acv', stiffness, gathered, precision=HIGH)]
    ppermute x20 -> x0, waiting for transfers between devices: 9.41 us -> none  [the longest x10 5.36 us: extended(): lax.ppermute(lax.slice_in_dim(block, block.shape[dim] - width, None, axis...]
  transfers between devices with their start and end apart: 21 -> 0, of which waited for: 13 -> 0; matrix products, arithmetic and copies ran while one was open for 2% -> 0% of each run, Pallas kernels for 0% -> 0%
where the time goes in v1:
time: 187 us
  Pallas kernels  174 us (93%)
  local copies, waits for them, and re-layouts  10.1 us (5%)
  between operations  2.66 us (1%)
    pallas_call x1, Pallas kernels, filtered_and_grams(): pl.pallas_call(functools.partial(filter_kernel, n_dom, n_grp), out_shape=...  155 us
    pallas_call x1, Pallas kernels, body(): pl.pallas_call(functools.partial(finish_kernel, rows_grid), out_shape=(ja...  19.3 us
    unnamed x21, local copies, waits for them, and re-layouts  5.23 us

profile of v1, /device:TPU:1, one launch (start us, length us, event | category | flops | bytes accessed | tf_op | source)
XLA Modules:
  0.0 187.0 jit_solution(12817654082100628620)
XLA Ops:
  2.6 0.0 copy-start.5
  2.6 0.0 copy-start.8
  2.6 0.7 copy-done.8
  3.3 0.0 copy-start.7
  3.3 0.7 copy-done.7
  4.0 0.0 copy-done.5
  4.0 0.6 pad.8.kmat_ref
  4.6 0.8 broadcast_in_dim.10.scale_ref
  5.3 0.0 copy-done.3
  5.3 0.1 copy.13
  5.5 0.1 select_select_fusion
  5.6 0.0 copy-done.4
  5.6 0.9 copy.24
  6.4 1.1 copy.19
  7.5 0.3 copy.18
  7.8 0.9 broadcast_in_dim_reshape.4.connr_ref
  8.7 0.0 copy-done.6
  8.7 1.3 broadcast_in_dim.8.pot_ref
  10.0 154.8 %shard_map.104 = (f32[2048,128]{1,0:T(8,128)}, f32[128,128]{1,0:T(8,128)}, f32[128,128]{1,0:T(8,128)}) custom-call(f32[1]{0:T(128)S(6)} %copy.26.cut_ref, f32[1]{0:T(128)S(6)} %copy.27.top_ref, s32[1]{0:T(128)} %copy.25.live_ref, f32[2048,128]{1,0:T(8,128)} %states_ref.1, f32[2048,128]{1,0:T(8,128)} %broadcast_in_dim.8.pot_ref, ...), custom_call_target="tpu_custom_call" | custom-call | tf_op jit(solution)/shard_map/pallas_call | solution.py:328
  164.8 0.0 copy-start
  164.8 1.2 copy-done
  166.0 0.8 copy-done.1
  166.9 0.8 copy-done.2
  167.7 19.3 %shard_map.105 = (f32[2048,128]{1,0:T(8,128)}, f32[32,32]{1,0:T(8,128)}) custom-call(f32[2048,128]{1,0:T(8,128)S(1)} %copy-done, f32[128,128]{1,0:T(8,128)S(1)} %copy-done.1, f32[128,128]{1,0:T(8,128)S(1)} %copy-done.2), custom_call_target="tpu_custom_call" | custom-call | tf_op jit(solution)/shard_map/pallas_call | solution.py:474
  (9 shorter events, 0.0 us)
Async XLA Ops:
  2.6 1.4 copy-start.5
  2.6 0.7 copy-start.8
  3.3 0.7 copy-start.7
  4.0 1.6 copy-start.4
  4.6 0.8 copy-start.3
  7.8 0.9 copy-start.6
  164.8 1.2 copy-start
  166.0 0.8 copy-start.1
  166.9 0.8 copy-start.2

commit v2 on v0

v2 whole, which is shorter than its diff:
```python
import functools

import jax
import jax.numpy as jnp
from jax import lax
from jax.experimental import pallas as pl
from jax.experimental.pallas import tpu as pltpu
from jax.sharding import PartitionSpec as P

NB = 8
NS = 128
NPC = 27
SLOTS = 28
DEG = 4
COUNT = 2048
FACE = 256
BLOCKS = 8
GROUPS = 4
GROWS = SLOTS * 8
ROWS = GROUPS * GROWS
WIN = 2 * FACE
GHOST = 2 * FACE

F32 = jnp.float32
BF16 = jnp.bfloat16
MESH = pl.DeviceIdType.MESH


def dot(a, b, dims=((1,), (0,))):
    return lax.dot_general(a, b, (dims, ((), ())), preferred_element_type=F32)


def split(x):
    hi = x.astype(BF16)
    lo = (x - hi.astype(F32)).astype(BF16)
    return jnp.concatenate([hi, lo], axis=1)


def halves(x):
    return x[:, :NS] + x[:, NS:]


def quarters(x):
    return (x[:NS, :NS] + x[NS:, NS:]) + (x[:NS, NS:] + x[NS:, :NS])


CHUNK_BLOCKS = ((0, 1), (0, 2), (1, 3), (2, 4), (3, 5), (4, 6), (5, 8), (6, 8))
CHUNK_AT = (0, 1, 3, 5, 7, 9, 11, 14)
CHUNK_ALL = 16


class Sum:
    def __init__(self, n_dom, n_grp, dom, grp, refs):
        self.src, self.slots, self.part, self.doms, self.out, self.sems1, self.sems2, self.sems3 = refs
        self.n_dom, self.n_grp, self.dom, self.grp = n_dom, n_grp, dom, grp

    def grp_copy(self, s, src, dst, sems):
        return pltpu.make_async_remote_copy(
            src_ref=src, dst_ref=dst, send_sem=sems.at[0, s], recv_sem=sems.at[1, s],
            device_id=(self.dom, lax.rem(self.grp + s, self.n_grp)), device_id_type=MESH,
        )

    def first(self):
        return [
            self.grp_copy(s, self.src.at[lax.rem(self.grp + s, self.n_grp)], self.slots.at[s], self.sems1)
            for s in range(1, self.n_grp)
        ]

    def second(self):
        return [
            pltpu.make_async_remote_copy(
                src_ref=self.part.at[0], dst_ref=self.doms.at[self.dom],
                send_sem=self.sems2.at[0, s], recv_sem=self.sems2.at[1, s],
                device_id=(lax.rem(self.dom + s, self.n_dom), self.grp), device_id_type=MESH,
            )
            for s in range(1, self.n_dom)
        ]

    def third(self):
        return [
            self.grp_copy(s, self.part.at[1], self.out.at[self.grp], self.sems3)
            for s in range(1, self.n_grp)
        ]

    def start_first(self, value):
        piece = NS // self.n_grp
        for j in range(self.n_grp):
            self.src[j] = value[j * piece : (j + 1) * piece]
        for copy in self.first():
            copy.start()
        self.slots[0] = self.src[self.grp]

    def start_second(self):
        for copy in self.first():
            copy.wait()
        self.part[0] = jnp.sum(self.slots[...], axis=0)
        for copy in self.second():
            copy.start()
        self.doms[self.dom] = self.part[0]

    def start_third(self):
        for copy in self.second():
            copy.wait()
        self.part[1] = jnp.sum(self.doms[...], axis=0)
        for copy in self.third():
            copy.start()
        self.out[self.grp] = self.part[1]

    def finish(self):
        for copy in self.third():
            copy.wait()
        return self.out[...].reshape(NS, NS)


def triple(x):
    hi = x.astype(BF16).astype(F32)
    rest = x - hi
    mid = rest.astype(BF16).astype(F32)
    return hi, mid, rest - mid


def factor_panel(p, left_ref, right_ref):
    sub = lax.broadcasted_iota(jnp.int32, (8, NS), 0)
    rows = slice(8 * p, 8 * p + 8)
    a = left_ref[rows]
    m = right_ref[rows]
    cols = [jnp.broadcast_to(a[:, 8 * p + k : 8 * p + k + 1], (8, NS)) for k in range(8)]
    pivots = jnp.ones((8, NS), F32)
    for j in range(8):
        at = [None] * j + [jnp.broadcast_to(cols[k][j : j + 1], (8, NS)) for k in range(j, 8)]
        mult = jnp.where(sub > j, cols[j] * (1.0 / at[j]), 0.0)
        for k in range(j + 1, 8):
            cols[k] = cols[k] - mult * at[k]
        a, m = (
            a - mult * jnp.broadcast_to(a[j : j + 1], (8, NS)),
            m - mult * jnp.broadcast_to(m[j : j + 1], (8, NS)),
        )
        pivots = jnp.where(sub == j, at[j], pivots)
    scale = 1.0 / jnp.sqrt(pivots)
    a, m = a * scale, m * scale
    right_ref[rows] = m
    if 8 * p + 8 < NS:
        hi, mid, low = triple(a)
        mhi, mmid, mlow = triple(m)
        one = jnp.concatenate([hi, hi, mid, hi, low, mid], axis=0).astype(BF16)
        two = jnp.concatenate([hi, mid, hi, low, hi, mid], axis=0)
        two_m = jnp.concatenate([mhi, mmid, mhi, mlow, mhi, mmid], axis=0)
        two = jnp.concatenate([two, two_m], axis=1).astype(BF16)
        both = dot(one, two, ((0,), (0,)))
        rest = slice(8 * p + 8, NS)
        left_ref[rest] = left_ref[rest] - both[rest, :NS]
        right_ref[rest] = right_ref[rest] - both[rest, NS:]


def filter_kernel(
    n_dom,
    n_grp,
    cut_ref,
    top_ref,
    live_ref,
    states_ref,
    pot_ref,
    scale_ref,
    kmat_ref,
    conn_ref,
    face_ref,
    ortho_ref,
    tile_ref,
    g_own,
    g_gho,
    t_own,
    t_gho,
    pick,
    pick_t,
    cross,
    kk,
    gath,
    loc,
    ext,
    extg,
    cur,
    prev,
    pot,
    scale,
    face_part,
    face_send,
    face_recv,
    back_send,
    back_recv,
    left,
    right,
    face_sems,
    back_sems,
    *sums,
):
    dom = lax.axis_index("dom")
    grp = lax.axis_index("grp")
    total = n_dom * n_grp
    me = dom * n_grp + grp
    up = lax.rem(me + 1, total)
    down = lax.rem(me + total - 1, total)
    up_id = (up // n_grp, lax.rem(up, n_grp))
    down_id = (down // n_grp, lax.rem(down, n_grp))
    partners = [up_id, down_id]
    partners += [(dom, lax.rem(grp + s, n_grp)) for s in range(1, n_grp)]
    partners += [(lax.rem(dom + s, n_dom), grp) for s in range(1, n_dom)]
    barrier = pltpu.get_barrier_semaphore()
    for device in partners:
        pl.semaphore_signal(barrier, inc=1, device_id=device, device_id_type=MESH)
    corr_sum = Sum(n_dom, n_grp, dom, grp, sums[: len(sums) // 2])
    gram_sum = Sum(n_dom, n_grp, dom, grp, sums[len(sums) // 2 :])

    def pair(send, recv, sems):
        return (
            pltpu.make_async_remote_copy(
                src_ref=send.at[0], dst_ref=recv.at[1],
                send_sem=sems.at[0], recv_sem=sems.at[1],
                device_id=down_id, device_id_type=MESH,
            ),
            pltpu.make_async_remote_copy(
                src_ref=send.at[1], dst_ref=recv.at[0],
                send_sem=sems.at[2], recv_sem=sems.at[3],
                device_id=up_id, device_id_type=MESH,
            ),
        )

    def send_faces(values):
        face_send[0] = values[:FACE]
        face_send[1] = values[FACE:]
        for copy in pair(face_send, face_recv, face_sems):
            copy.start()

    def received(recv):
        low = jnp.where(me == 0, 0.0, recv[0])
        high = jnp.where(me == total - 1, 0.0, recv[1])
        return low, high

    live = live_ref[0]
    face_rows = jnp.concatenate([face_ref[:, :NS], face_ref[:, NS:]], axis=0).astype(F32)
    stacked = jnp.concatenate(
        [pot_ref[...], scale_ref[...], face_rows, jnp.zeros((2, NS), F32)], axis=0
    )
    columns = stacked.T
    for i, c in enumerate((18, 20, 19, 21)):
        want = columns[:, c : c + 1].astype(jnp.int32)
        lane = lax.broadcasted_iota(jnp.int32, (NS, COUNT), 1)
        pick[i * NS : (i + 1) * NS] = jnp.where(want == lane, 1.0, 0.0).astype(BF16)
    for i in range(0, COUNT, FACE):
        at = slice(i, i + FACE)
        node = lax.broadcasted_iota(jnp.int32, (FACE, NS), 0) + i
        cur[at] = jnp.where(node < live, states_ref[at], 0.0)
        ext[at] = split(cur[at])
    face_part[...] = halves(dot(pick[...], ext[...]))
    pl.semaphore_wait(barrier, len(partners))
    send_faces(face_part[...])

    conn = conn_ref[...]
    conn_col = conn.astype(F32).T.astype(jnp.int32)
    for b in range(BLOCKS):
        col = conn_col[:, b : b + 1]
        lane = lax.broadcasted_iota(jnp.int32, (ROWS, WIN), 1)
        g_own[b] = jnp.where(col == lane, 1.0, 0.0).astype(BF16)
        g_gho[b] = jnp.where(col == lane + WIN, 1.0, 0.0).astype(BF16)
        sub = lax.broadcasted_iota(jnp.int32, (GHOST, ROWS), 0)
        t_gho[:, b * ROWS : (b + 1) * ROWS] = jnp.where(conn[b : b + 1] == sub + WIN, 1.0, 0.0).astype(
            BF16
        )
    for j, (first, last) in enumerate(CHUNK_BLOCKS):
        for b in range(first, last):
            sub = lax.broadcasted_iota(jnp.int32, (FACE, ROWS), 0) + (j - min(b, 6)) * FACE
            at = CHUNK_AT[j] + b - first
            t_own[:, at * ROWS : (at + 1) * ROWS] = jnp.where(conn[b : b + 1] == sub, 1.0, 0.0).astype(
                BF16
            )
    for half_face in range(2):
        sub = lax.broadcasted_iota(jnp.int32, (COUNT, FACE), 0)
        pick_t[:, half_face * FACE : (half_face + 1) * FACE] = jnp.where(
            face_ref[half_face : half_face + 1] == sub, 1.0, 0.0
        ).astype(BF16)
    cross[...] = dot(pick[...], pick_t[...]).astype(BF16)
    spread = (
        lax.broadcasted_iota(jnp.int32, (GROWS, NPC), 0) // 8
        == lax.broadcasted_iota(jnp.int32, (GROWS, NPC), 1)
    )
    spread = jnp.where(spread, 1.0, 0.0).astype(F32)
    wide = lax.dot_general(
        spread, kmat_ref[...], (((1,), (0,)), ((), ())),
        precision=lax.Precision.HIGHEST, preferred_element_type=F32,
    )
    wide = lax.dot_general(
        wide, spread, (((1,), (1,)), ((), ())),
        precision=lax.Precision.HIGHEST, preferred_element_type=F32,
    )
    same = lax.rem(lax.broadcasted_iota(jnp.int32, (GROWS, GROWS), 0), 8) == lax.rem(
        lax.broadcasted_iota(jnp.int32, (GROWS, GROWS), 1), 8
    )
    wide = jnp.where(same, wide, 0.0)
    kk[0] = wide.astype(BF16)
    kk[1] = (wide - wide.astype(BF16).astype(F32)).astype(BF16)
    for i in range(COUNT // NS):
        pot[i * NS : (i + 1) * NS] = jnp.broadcast_to(columns[:, i : i + 1], (NS, NS))
    for i in range(2):
        cell = lax.broadcasted_iota(jnp.int32, (NS, NS), 0) + i * NS
        value = jnp.broadcast_to(columns[:, 16 + i : 17 + i], (NS, NS))
        scale[i * NS : (i + 1) * NS] = jnp.where(8 * cell + 8 <= live, value, 0.0)
    prev[...] = jnp.zeros((COUNT, NS), F32)
    span = (top_ref[0] - cut_ref[0]) * 0.5
    centre = (top_ref[0] + cut_ref[0]) * 0.5

    def gather_owned():
        for b in range(BLOCKS):
            at = min(b, 6) * FACE
            gath[b] = dot(g_own[b], ext[at : at + WIN]).astype(BF16)

    def gather_ghosts():
        for b in range(BLOCKS):
            gath[b] = gath[b] + dot(g_gho[b], extg[...]).astype(BF16)

    def take_faces():
        for copy in pair(face_send, face_recv, face_sems):
            copy.wait()
        low, high = received(face_recv)
        extg[:FACE] = split(low)
        extg[FACE:] = split(high)

    def apply_cells():
        for b in range(BLOCKS):
            for i in range(0, GROUPS, 2):
                one = gath[b, i * GROWS : (i + 1) * GROWS]
                two = gath[b, (i + 1) * GROWS : (i + 2) * GROWS]
                low = dot(kk[1], jnp.concatenate([one[:, :NS], two[:, :NS]], axis=1))
                for j, part in enumerate((one, two)):
                    r = b * GROUPS + i + j
                    out = halves(dot(kk[0], part)) + low[:, j * NS : (j + 1) * NS]
                    out = (out.reshape(SLOTS, 8, NS) * scale[r * 8 : r * 8 + 8][None]).reshape(GROWS, NS)
                    loc[r * GROWS : (r + 1) * GROWS] = split(out)

    def step(k, carry):
        alpha = jnp.where(k == 0, 1.0, 2.0) / span
        beta = jnp.where(k == 0, 0.0, 1.0)
        gather_owned()
        take_faces()
        gather_ghosts()
        apply_cells()
        back = halves(dot(t_gho[...], loc[...]))
        back_send[0] = back[:FACE]
        back_send[1] = back[FACE:]
        for copy in pair(back_send, back_recv, back_sems):
            copy.start()
        for j, (first, last) in enumerate(CHUNK_BLOCKS):
            at = slice(j * FACE, (j + 1) * FACE)
            lanes = slice(CHUNK_AT[j] * ROWS, (CHUNK_AT[j] + last - first) * ROWS)
            added = halves(dot(t_own[:, lanes], loc[first * ROWS : last * ROWS]))
            now = cur[at]
            new = alpha * (added + (pot[at] - centre) * now) - beta * prev[at]
            prev[at] = now
            cur[at] = new
            ext[at] = split(new)
        face_part[...] = halves(dot(pick[...], ext[...]))
        for copy in pair(back_send, back_recv, back_sems):
            copy.wait()
        low, high = received(back_recv)
        extg[:FACE] = split(alpha * low)
        extg[FACE:] = split(alpha * high)
        send_faces(face_part[...] + halves(dot(cross[...], extg[...])))
        for j in range(COUNT // FACE):
            at = slice(j * FACE, (j + 1) * FACE)
            new = cur[at] + halves(dot(pick_t[at], extg[...]))
            cur[at] = new
            ext[at] = split(new)
        return carry

    lax.fori_loop(0, DEG, step, 0)

    share = 1.0 / (total * COUNT)
    corr_sum.start_first(quarters(dot(ext[...], ext[...], ((0,), (0,)))) * share)
    gather_owned()
    take_faces()
    corr_sum.start_second()
    gather_ghosts()
    apply_cells()
    corr_sum.start_third()
    gram = jnp.zeros((2 * NS, 2 * NS), F32)
    for b in range(BLOCKS):
        gram = gram + dot(gath[b], loc[b * ROWS : (b + 1) * ROWS], ((0,), (0,)))
    for j in range(COUNT // FACE):
        at = slice(j * FACE, (j + 1) * FACE)
        gram = gram + dot(ext[at], split(pot[at] * cur[at]), ((0,), (0,)))
    gram_sum.start_first(quarters(gram) * share)
    left[...] = corr_sum.finish()
    right[...] = jnp.where(
        lax.broadcasted_iota(jnp.int32, (NS, NS), 0) == lax.broadcasted_iota(jnp.int32, (NS, NS), 1),
        1.0,
        0.0,
    ).astype(F32)
    for p in range(6):
        factor_panel(p, left, right)
    gram_sum.start_second()
    for p in range(6, NS // 8):
        factor_panel(p, left, right)
    gram_sum.start_third()
    inv = right[...]
    hi = inv.astype(BF16)
    low = (inv - hi.astype(F32)).astype(BF16)
    wide = jnp.concatenate([hi, hi], axis=1)
    narrow = jnp.concatenate([low, jnp.zeros_like(low)], axis=1)
    weights = jnp.concatenate([wide, narrow], axis=0)
    for j in range(COUNT // FACE):
        at = slice(j * FACE, (j + 1) * FACE)
        ortho_ref[at] = halves(dot(ext[at], weights, ((1,), (1,))))
    hgram = gram_sum.finish()
    rows_grid = n_grp // 4
    high = lax.Precision.HIGHEST
    r = grp // 4
    q = lax.rem(grp, 4)
    jump = 8 * rows_grid
    mine = jnp.concatenate(
        [right[pl.ds(pl.multiple_of(jump * t + 8 * r, 8), 8)] for t in range(NS // jump)], axis=0
    )
    other = jnp.concatenate(
        [right[pl.ds(pl.multiple_of(32 * t + 8 * q, 8), 8)] for t in range(NS // 32)], axis=0
    )
    mine = jnp.dot(mine, hgram, precision=high, preferred_element_type=F32)
    tile_ref[...] = lax.dot_general(
        mine, other, (((1,), (1,)), ((), ())), precision=high, preferred_element_type=F32
    )


def whole(n_dom, n_grp, operands):
    piece = NS // n_grp
    rows_grid = n_grp // 4
    vmem = pl.BlockSpec(memory_space=pltpu.VMEM)
    smem = pl.BlockSpec(memory_space=pltpu.SMEM)
    dma = pltpu.SemaphoreType.DMA
    one_sum = [
        pltpu.VMEM((n_grp, piece, NS), F32),
        pltpu.VMEM((n_grp, piece, NS), F32),
        pltpu.VMEM((2, piece, NS), F32),
        pltpu.VMEM((n_dom, piece, NS), F32),
        pltpu.VMEM((n_grp, piece, NS), F32),
        dma((2, n_grp)),
        dma((2, n_dom)),
        dma((2, n_grp)),
    ]
    faces = pltpu.VMEM((2, FACE, NS), F32)
    field = pltpu.VMEM((COUNT, NS), F32)
    return pl.pallas_call(
        functools.partial(filter_kernel, n_dom, n_grp),
        out_shape=(
            jax.ShapeDtypeStruct((COUNT, NS), F32),
            jax.ShapeDtypeStruct((NS // rows_grid, NS // 4), F32),
        ),
        in_specs=[smem] * 3 + [vmem] * 6,
        out_specs=(vmem, vmem),
        scratch_shapes=[
            pltpu.VMEM((BLOCKS, ROWS, WIN), BF16),
            pltpu.VMEM((BLOCKS, ROWS, GHOST), BF16),
            pltpu.VMEM((FACE, CHUNK_ALL * ROWS), BF16),
            pltpu.VMEM((GHOST, BLOCKS * ROWS), BF16),
            pltpu.VMEM((2 * FACE, COUNT), BF16),
            pltpu.VMEM((COUNT, 2 * FACE), BF16),
            pltpu.VMEM((2 * FACE, 2 * FACE), BF16),
            pltpu.VMEM((2, GROWS, GROWS), BF16),
            pltpu.VMEM((BLOCKS, ROWS, 2 * NS), BF16),
            pltpu.VMEM((BLOCKS * ROWS, 2 * NS), BF16),
            pltpu.VMEM((COUNT, 2 * NS), BF16),
            pltpu.VMEM((GHOST, 2 * NS), BF16),
            field,
            field,
            field,
            pltpu.VMEM((2 * NS, NS), F32),
            pltpu.VMEM((2 * FACE, NS), F32),
            faces,
            faces,
            faces,
            faces,
            pltpu.VMEM((NS, NS), F32),
            pltpu.VMEM((NS, NS), F32),
            dma((4,)),
            dma((4,)),
            *one_sum,
            *one_sum,
        ],
        compiler_params=pltpu.CompilerParams(
            collective_id=0, has_side_effects=True, vmem_limit_bytes=62 * 1024 * 1024
        ),
    )(*operands)


def body(
    states,
    potential,
    cell_scale,
    stiffness,
    connect,
    face_nodes,
    node_count,
    filter_cut,
    spectrum_top,
):
    cells = cell_scale.shape[0]
    start = jnp.minimum(jnp.arange(cells, dtype=jnp.int32) // 32, 6) * FACE
    column = jnp.where(
        connect < FACE,
        connect + WIN,
        jnp.where(connect >= FACE + COUNT, connect - FACE - COUNT + WIN + FACE, connect - FACE - start),
    )
    column = jnp.pad(column, ((0, SLOTS - NPC), (0, 0)), constant_values=-1)
    column = column.reshape(SLOTS, BLOCKS, GROUPS, 8).transpose(1, 2, 0, 3).reshape(BLOCKS, ROWS)
    return whole(
        lax.axis_size("dom"),
        lax.axis_size("grp"),
        (
            filter_cut,
            spectrum_top,
            node_count,
            states,
            potential.reshape(COUNT // NS, NS),
            cell_scale.reshape(cells // NS, NS),
            stiffness,
            column,
            face_nodes,
        ),
    )


def solution(mesh):
    placed = (
        P(("dom", "grp"), None),
        P(("dom", "grp")),
        P(("dom", "grp")),
        P(),
        P(None, ("dom", "grp")),
        P(None, ("dom", "grp")),
        P(("dom", "grp")),
        P(),
        P(),
    )
    return jax.shard_map(
        body,
        mesh=mesh,
        in_specs=placed,
        out_specs=(P(("dom", "grp"), None), P("grp", None)),
        check_vma=False,
    )
```

time: 612 us -> 134 us (0.22)
  matrix products: 283 us -> 0 us
  waiting for transfers between devices: 191 us -> 0 us
  Pallas kernels: 0 us -> 126 us
  starting transfers between devices: 65.2 us -> 0 us
  other arithmetic: 31.7 us -> 0.11 us
  between operations: 18.6 us -> 2.61 us
  local copies, waits for them, and re-layouts: 18.5 us -> 4.91 us
    dot_general x145 -> x0, matrix products: 283 us -> none  [the longest x40 130 us: block_term(): contrib = jnp.dot(onehot.T, local.reshape(-1, width), precision=HIGH)]
    psum x1 -> x0, waiting for transfers between devices: 182 us -> none  [body(): lax.psum((correlation_part, hgram_part), ('dom', 'grp'))]
    pallas_call x0 -> x1, Pallas kernels: none -> 126 us  [whole(): pl.pallas_call(functools.partial(filter_kernel, n_dom, n_grp), out_shape=...]
    ppermute x20 -> x0, starting transfers between devices: 65.1 us -> none  [the longest x10 44.5 us: extended(): lax.ppermute(lax.slice_in_dim(block, block.shape[dim] - width, None, axis...]
    another operation x5 -> x0, other arithmetic: 22.9 us -> none  [the longest x3 12.4 us: body(): factor = jnp.linalg.cholesky(correlation)]
    mul x40 -> x0, local copies, waits for them, and re-layouts: 10.5 us -> none  [block_term(): jnp.einsum('ab,bcv->acv', stiffness, gathered, precision=HIGH)]
    ppermute x20 -> x0, waiting for transfers between devices: 9.41 us -> none  [the longest x10 5.36 us: extended(): lax.ppermute(lax.slice_in_dim(block, block.shape[dim] - width, None, axis...]
  transfers between devices with their start and end apart: 21 -> 0, of which waited for: 13 -> 0; matrix products, arithmetic and copies ran while one was open for 2% -> 0% of each run, Pallas kernels for 0% -> 0%
where the time goes in v2:
time: 134 us
  Pallas kernels  126 us (94%)
  local copies, waits for them, and re-layouts  4.91 us (4%)
  between operations  2.61 us (2%)
    pallas_call x1, Pallas kernels, whole(): pl.pallas_call(functools.partial(filter_kernel, n_dom, n_grp), out_shape=...  126 us
    unnamed x5, local copies, waits for them, and re-layouts  3.74 us

profile of v2, /device:TPU:1, one launch (start us, length us, event | category | flops | bytes accessed | tf_op | source)
XLA Modules:
  0.0 134.1 jit_solution(11859969990457108778)
XLA Ops:
  2.6 0.9 copy.12
  3.4 0.1 select_select_fusion
  3.6 0.3 copy.17
  3.9 0.9 reshape.34.conn_ref
  4.7 126.5 %shard_map.104 = (f32[2048,128]{1,0:T(8,128)}, f32[32,32]{1,0:T(8,128)}) custom-call(f32[1]{0:T(128)S(6)} %copy.21.cut_ref, f32[1]{0:T(128)S(6)} %copy.22.top_ref, s32[1]{0:T(128)S(6)} %copy.20.live_ref, f32[2048,128]{1,0:T(8,128)} %states_ref.1, f32[16,128]{1,0:T(8,128)} %bitcast.6, f32[2,128]{1,0:T(2,128)} %bitcast.7, f32[27,27]{1,0:T(8,128)} %kmat_ref.1, ...), custom_call_target="tpu_custom_call" | custom-call | tf_op jit(solution)/shard_map/pallas_call | solution.py:447
  131.2 0.0 copy-start
  131.2 2.3 %copy.23 = f32[2048,128]{1,0:T(8,128)} copy(f32[2048,128]{1,0:T(8,128)} %get-tuple-element.4) | data formatting | bytes 2097152
  133.5 0.0 copy-done
  133.5 0.6 copy.24
  (2 shorter events, 0.0 us)
Async XLA Ops:
  131.2 2.3 %copy-start = (f32[32,32]{1,0:T(8,128)S(1)}, f32[32,32]{1,0:T(8,128)}, u32[]{:S(2)}) copy-start(f32[32,32]{1,0:T(8,128)} %get-tuple-element.5) | copy-start | bytes 12292

commit v3 on v2

--- a/solution.py
+++ b/solution.py
@@ -10,6 +10,7 @@
 NB = 8
 NS = 128
 NPC = 27
+CELLS = 256
 SLOTS = 28
 DEG = 4
 COUNT = 2048
@@ -119,12 +120,11 @@
     return hi, mid, rest - mid
 
 
-def factor_panel(p, left_ref, right_ref):
+def factor_panel(p, left_ref, right_ref, inv_ref):
     sub = lax.broadcasted_iota(jnp.int32, (8, NS), 0)
-    rows = slice(8 * p, 8 * p + 8)
-    a = left_ref[rows]
-    m = right_ref[rows]
-    cols = [jnp.broadcast_to(a[:, 8 * p + k : 8 * p + k + 1], (8, NS)) for k in range(8)]
+    a = left_ref[:8]
+    m = right_ref[:8]
+    cols = [jnp.broadcast_to(a[:, k : k + 1], (8, NS)) for k in range(8)]
     pivots = jnp.ones((8, NS), F32)
     for j in range(8):
         at = [None] * j + [jnp.broadcast_to(cols[k][j : j + 1], (8, NS)) for k in range(j, 8)]
@@ -138,18 +138,19 @@
         pivots = jnp.where(sub == j, at[j], pivots)
     scale = 1.0 / jnp.sqrt(pivots)
     a, m = a * scale, m * scale
-    right_ref[rows] = m
-    if 8 * p + 8 < NS:
-        hi, mid, low = triple(a)
-        mhi, mmid, mlow = triple(m)
-        one = jnp.concatenate([hi, hi, mid, hi, low, mid], axis=0).astype(BF16)
-        two = jnp.concatenate([hi, mid, hi, low, hi, mid], axis=0)
-        two_m = jnp.concatenate([mhi, mmid, mhi, mlow, mhi, mmid], axis=0)
-        two = jnp.concatenate([two, two_m], axis=1).astype(BF16)
-        both = dot(one, two, ((0,), (0,)))
-        rest = slice(8 * p + 8, NS)
-        left_ref[rest] = left_ref[rest] - both[rest, :NS]
-        right_ref[rest] = right_ref[rest] - both[rest, NS:]
+    inv_ref[pl.ds(pl.multiple_of(8 * p, 8), 8)] = m
+    a = jnp.concatenate([a[:, 8:], jnp.zeros((8, 8), F32)], axis=1)
+    hi, mid, low = triple(a)
+    mhi, mmid, mlow = triple(m)
+    one = jnp.concatenate([hi, hi, mid, hi, low, mid], axis=0).astype(BF16)
+    two = jnp.concatenate([hi, mid, hi, low, hi, mid], axis=0)
+    two_m = jnp.concatenate([mhi, mmid, mhi, mlow, mhi, mmid], axis=0)
+    two = jnp.concatenate([two, two_m], axis=1).astype(BF16)
+    both = dot(one, two, ((0,), (0,)))[: NS - 8]
+    rest = left_ref[8:]
+    rest = jnp.concatenate([rest[:, 8:], jnp.zeros((NS - 8, 8), F32)], axis=1)
+    left_ref[: NS - 8] = rest - both[:, :NS]
+    right_ref[: NS - 8] = right_ref[8:] - both[:, NS:]
 
 
 def filter_kernel(
@@ -178,6 +179,8 @@
     loc,
     ext,
     extg,
+    extr,
+    a_far,
     cur,
     prev,
     pot,
@@ -189,6 +192,11 @@
     back_recv,
     left,
     right,
+    inverse,
+    conn_col,
+    conn_row,
+    far_part,
+    gram_acc,
     face_sems,
     back_sems,
     *sums,
@@ -199,9 +207,12 @@
     me = dom * n_grp + grp
     up = lax.rem(me + 1, total)
     down = lax.rem(me + total - 1, total)
-    up_id = (up // n_grp, lax.rem(up, n_grp))
-    down_id = (down // n_grp, lax.rem(down, n_grp))
-    partners = [up_id, down_id]
+    even = lax.rem(grp, 2) == 0
+    near_at = jnp.where(even, up, down)
+    far_at = jnp.where(even, down, up)
+    ids = [(at // n_grp, lax.rem(at, n_grp)) for at in (near_at, far_at)]
+    edge = jnp.logical_or(me == 0, me == total - 1)
+    partners = list(ids)
     partners += [(dom, lax.rem(grp + s, n_grp)) for s in range(1, n_grp)]
     partners += [(lax.rem(dom + s, n_dom), grp) for s in range(1, n_dom)]
     barrier = pltpu.get_barrier_semaphore()
@@ -210,73 +221,114 @@
     corr_sum = Sum(n_dom, n_grp, dom, grp, sums[: len(sums) // 2])
     gram_sum = Sum(n_dom, n_grp, dom, grp, sums[len(sums) // 2 :])
 
-    def pair(send, recv, sems):
-        return (
-            pltpu.make_async_remote_copy(
-                src_ref=send.at[0], dst_ref=recv.at[1],
-                send_sem=sems.at[0], recv_sem=sems.at[1],
-                device_id=down_id, device_id_type=MESH,
-            ),
-            pltpu.make_async_remote_copy(
-                src_ref=send.at[1], dst_ref=recv.at[0],
-                send_sem=sems.at[2], recv_sem=sems.at[3],
-                device_id=up_id, device_id_type=MESH,
-            ),
+    def swap(side, send, recv, sems):
+        return pltpu.make_async_remote_copy(
+            src_ref=send.at[side], dst_ref=recv.at[side],
+            send_sem=sems.at[side, 0], recv_sem=sems.at[side, 1],
+            device_id=ids[side], device_id_type=MESH,
         )
 
     def send_faces(values):
-        face_send[0] = values[:FACE]
-        face_send[1] = values[FACE:]
-        for copy in pair(face_send, face_recv, face_sems):
-            copy.start()
-
-    def received(recv):
-        low = jnp.where(me == 0, 0.0, recv[0])
-        high = jnp.where(me == total - 1, 0.0, recv[1])
-        return low, high
+        for side in (1, 0):
+            face_send[side] = values[side * FACE : (side + 1) * FACE]
+            swap(side, face_send, face_recv, face_sems).start()
+
+    def take_face(side):
+        swap(side, face_send, face_recv, face_sems).wait()
+        value = face_recv[side] if side == 0 else jnp.where(edge, 0.0, face_recv[side])
+        extg[side * FACE : (side + 1) * FACE] = split(value)
+
+    def send_back(side, value):
+        back_send[side] = value
+        swap(side, back_send, back_recv, back_sems).start()
+
+    def take_back(side, alpha):
+        swap(side, back_send, back_recv, back_sems).wait()
+        value = back_recv[side] if side == 0 else jnp.where(edge, 0.0, back_recv[side])
+        extr[side * FACE : (side + 1) * FACE] = split(alpha * value)
 
     live = live_ref[0]
-    face_rows = jnp.concatenate([face_ref[:, :NS], face_ref[:, NS:]], axis=0).astype(F32)
+    lower, upper = face_ref[0:1], face_ref[1:2]
+    faces = [jnp.where(even, upper, lower), jnp.where(even, lower, upper)]
+    face_rows = jnp.concatenate(
+        [faces[0][:, :NS], faces[0][:, NS:], faces[1][:, :NS], faces[1][:, NS:]], axis=0
+    ).astype(F32)
     stacked = jnp.concatenate(
         [pot_ref[...], scale_ref[...], face_rows, jnp.zeros((2, NS), F32)], axis=0
     )
     columns = stacked.T
-    for i, c in enumerate((18, 20, 19, 21)):
-        want = columns[:, c : c + 1].astype(jnp.int32)
-        lane = lax.broadcasted_iota(jnp.int32, (NS, COUNT), 1)
-        pick[i * NS : (i + 1) * NS] = jnp.where(want == lane, 1.0, 0.0).astype(BF16)
-    for i in range(0, COUNT, FACE):
-        at = slice(i, i + FACE)
-        node = lax.broadcasted_iota(jnp.int32, (FACE, NS), 0) + i
-        cur[at] = jnp.where(node < live, states_ref[at], 0.0)
-        ext[at] = split(cur[at])
+    wants = jnp.concatenate([columns[:, c : c + 1] for c in (18, 19, 20, 21)], axis=0).astype(jnp.int32)
+    wants = jnp.broadcast_to(wants, (2 * FACE, NS))
+
+    def first_field(i, carry):
+        start = pl.multiple_of(i * NS, NS)
+        at = pl.ds(start, NS)
+        node = lax.broadcasted_iota(jnp.int32, (NS, NS), 0) + start
+        value = jnp.where(node < live, states_ref[at], 0.0)
+        cur[at] = value
+        prev[at] = jnp.zeros((NS, NS), F32)
+        ext[at] = split(value)
+        lane = lax.broadcasted_iota(jnp.int32, (2 * FACE, NS), 1) + start
+        pick[:, at] = jnp.where(wants == lane, 1.0, 0.0).astype(BF16)
+        return carry
+
+    lax.fori_loop(0, COUNT // NS, first_field, 0)
     face_part[...] = halves(dot(pick[...], ext[...]))
+
+    raw = jnp.concatenate([conn_ref[...], jnp.full((32 - NPC, CELLS), -1, jnp.int32)], axis=0)
+    cell = lax.broadcasted_iota(jnp.int32, (32, CELLS), 1)
+    start = jnp.minimum(cell // 32, 6) * FACE
+    low_at = WIN + jnp.where(even, FACE, 0)
+    high_at = WIN + jnp.where(even, 0, FACE)
+    column = jnp.where(
+        raw < FACE,
+        raw + low_at,
+        jnp.where(raw >= FACE + COUNT, raw - (FACE + COUNT) + high_at, raw - FACE - start),
+    )
+    column = jnp.where(raw < 0, -1, column)
+    by_cell = column.astype(F32).T
+    lane = lax.broadcasted_iota(jnp.int32, (ROWS, NS), 1)
+    packed = jnp.zeros((ROWS, NS), F32)
+    for b in range(BLOCKS):
+        pieces = []
+        for r in range(b * GROUPS, (b + 1) * GROUPS):
+            pieces += [by_cell[8 * r : 8 * r + 8, a : a + 1] for a in range(SLOTS)]
+        col = jnp.concatenate([jnp.broadcast_to(piece, (8, NS)) for piece in pieces], axis=0)
+        conn_col[b] = col.astype(jnp.int32)
+        packed = jnp.where(lane == b, col, packed)
+    conn_row[...] = packed.T[:BLOCKS].astype(jnp.int32)
+
     pl.semaphore_wait(barrier, len(partners))
     send_faces(face_part[...])
 
-    conn = conn_ref[...]
-    conn_col = conn.astype(F32).T.astype(jnp.int32)
-    for b in range(BLOCKS):
-        col = conn_col[:, b : b + 1]
+    def build(b, carry):
+        col = conn_col[b]
+        col = jnp.concatenate([col] * (WIN // NS), axis=1)
         lane = lax.broadcasted_iota(jnp.int32, (ROWS, WIN), 1)
         g_own[b] = jnp.where(col == lane, 1.0, 0.0).astype(BF16)
         g_gho[b] = jnp.where(col == lane + WIN, 1.0, 0.0).astype(BF16)
-        sub = lax.broadcasted_iota(jnp.int32, (GHOST, ROWS), 0)
-        t_gho[:, b * ROWS : (b + 1) * ROWS] = jnp.where(conn[b : b + 1] == sub + WIN, 1.0, 0.0).astype(
-            BF16
-        )
-    for j, (first, last) in enumerate(CHUNK_BLOCKS):
-        for b in range(first, last):
-            sub = lax.broadcasted_iota(jnp.int32, (FACE, ROWS), 0) + (j - min(b, 6)) * FACE
-            at = CHUNK_AT[j] + b - first
-            t_own[:, at * ROWS : (at + 1) * ROWS] = jnp.where(conn[b : b + 1] == sub, 1.0, 0.0).astype(
-                BF16
-            )
-    for half_face in range(2):
-        sub = lax.broadcasted_iota(jnp.int32, (COUNT, FACE), 0)
-        pick_t[:, half_face * FACE : (half_face + 1) * FACE] = jnp.where(
-            face_ref[half_face : half_face + 1] == sub, 1.0, 0.0
-        ).astype(BF16)
+        row = conn_row[pl.ds(b, 1)]
+        sub = lax.broadcasted_iota(jnp.int32, (WIN, ROWS), 0)
+        gho = jnp.where(row == sub + WIN, 1.0, 0.0).astype(BF16)
+        t_gho[:, pl.ds(pl.multiple_of(b * ROWS, NS), ROWS)] = gho
+        own = jnp.where(row == sub, 1.0, 0.0).astype(BF16)
+        at = jnp.where(b < 7, 2 * b, 13)
+        t_own[:, pl.ds(pl.multiple_of(at * ROWS, NS), ROWS)] = own[:FACE]
+        at = jnp.where(b < 6, 2 * b + 1, b + 8)
+        t_own[:, pl.ds(pl.multiple_of(at * ROWS, NS), ROWS)] = own[FACE:]
+        return carry
+
+    lax.fori_loop(0, BLOCKS, build, 0)
+
+    def build_pick(i, carry):
+        start = pl.multiple_of(i * NS, NS)
+        sub = lax.broadcasted_iota(jnp.int32, (NS, FACE), 0) + start
+        for side in range(2):
+            value = jnp.where(faces[side] == sub, 1.0, 0.0).astype(BF16)
+            pick_t[pl.ds(start, NS), side * FACE : (side + 1) * FACE] = value
+        return carry
+
+    lax.fori_loop(0, COUNT // NS, build_pick, 0)
     cross[...] = dot(pick[...], pick_t[...]).astype(BF16)
     spread = (
         lax.broadcasted_iota(jnp.int32, (GROWS, NPC), 0) // 8
@@ -303,7 +355,6 @@
         cell = lax.broadcasted_iota(jnp.int32, (NS, NS), 0) + i * NS
         value = jnp.broadcast_to(columns[:, 16 + i : 17 + i], (NS, NS))
         scale[i * NS : (i + 1) * NS] = jnp.where(8 * cell + 8 <= live, value, 0.0)
-    prev[...] = jnp.zeros((COUNT, NS), F32)
     span = (top_ref[0] - cut_ref[0]) * 0.5
     centre = (top_ref[0] + cut_ref[0]) * 0.5
 
@@ -312,16 +363,17 @@
             at = min(b, 6) * FACE
             gath[b] = dot(g_own[b], ext[at : at + WIN]).astype(BF16)
 
-    def gather_ghosts():
+    def gather_side(side):
+        at = slice(side * FACE, (side + 1) * FACE)
         for b in range(BLOCKS):
-            gath[b] = gath[b] + dot(g_gho[b], extg[...]).astype(BF16)
-
-    def take_faces():
-        for copy in pair(face_send, face_recv, face_sems):
-            copy.wait()
-        low, high = received(face_recv)
-        extg[:FACE] = split(low)
-        extg[FACE:] = split(high)
+            gath[b] = gath[b] + dot(g_gho[b, :, at], extg[at]).astype(BF16)
+
+    def scatter_side(side):
+        return halves(dot(t_gho[side * FACE : (side + 1) * FACE], loc[...]))
+
+    def far_far():
+        values = extg[FACE:]
+        return halves(dot(a_far[0], values)) + dot(a_far[1], values[:, :NS])
 
     def apply_cells():
         for b in range(BLOCKS):
@@ -335,71 +387,121 @@
                     out = (out.reshape(SLOTS, 8, NS) * scale[r * 8 : r * 8 + 8][None]).reshape(GROWS, NS)
                     loc[r * GROWS : (r + 1) * GROWS] = split(out)
 
+    def build_far():
+        def far_block(h, carry):
+            for t in range(2):
+                b = 2 * h + t
+                for i in range(GROUPS):
+                    part = g_gho[b, i * GROWS : (i + 1) * GROWS, FACE:]
+                    out = dot(kk[0], part) + dot(kk[1], part)
+                    by = scale[pl.ds(pl.multiple_of(b * 8 * GROUPS + 8 * i, 8), 8)]
+                    by = jnp.concatenate([by, by], axis=1)
+                    out = (out.reshape(SLOTS, 8, FACE) * by[None]).reshape(GROWS, FACE)
+                    out_hi = out.astype(BF16)
+                    gath[b, i * GROWS : (i + 1) * GROWS] = out_hi
+                    loc[pl.ds(pl.multiple_of(b * ROWS + i * GROWS, 16), GROWS)] = (
+                        out - out_hi.astype(F32)
+                    ).astype(BF16)
+            return carry
+
+        lax.fori_loop(0, BLOCKS // 2, far_block, 0)
+        out = dot(t_gho[FACE:], gath[...].reshape(BLOCKS * ROWS, FACE)) + dot(t_gho[FACE:], loc[...])
+        a_far[0] = out.astype(BF16)
+        a_far[1] = (out - out.astype(BF16).astype(F32)).astype(BF16)
+
     def step(k, carry):
         alpha = jnp.where(k == 0, 1.0, 2.0) / span
         beta = jnp.where(k == 0, 0.0, 1.0)
+        @pl.when(k == DEG)
+        def _():
+            corr_sum.start_first(quarters(dot(ext[...], ext[...], ((0,), (0,)))) * share)
+
         gather_owned()
-        take_faces()
-        gather_ghosts()
+        take_face(0)
+        gather_side(0)
+
+        @pl.when(k == 0)
+        def _():
+            take_face(1)
+            gather_side(1)
+
         apply_cells()
-        back = halves(dot(t_gho[...], loc[...]))
-        back_send[0] = back[:FACE]
-        back_send[1] = back[FACE:]
-        for copy in pair(back_send, back_recv, back_sems):
-            copy.start()
-        for j, (first, last) in enumerate(CHUNK_BLOCKS):
-            at = slice(j * FACE, (j + 1) * FACE)
-            lanes = slice(CHUNK_AT[j] * ROWS, (CHUNK_AT[j] + last - first) * ROWS)
-            added = halves(dot(t_own[:, lanes], loc[first * ROWS : last * ROWS]))
-            now = cur[at]
-            new = alpha * (added + (pot[at] - centre) * now) - beta * prev[at]
-            prev[at] = now
-            cur[at] = new
-            ext[at] = split(new)
-        face_part[...] = halves(dot(pick[...], ext[...]))
-        for copy in pair(back_send, back_recv, back_sems):
-            copy.wait()
-        low, high = received(back_recv)
-        extg[:FACE] = split(alpha * low)
-        extg[FACE:] = split(alpha * high)
-        send_faces(face_part[...] + halves(dot(cross[...], extg[...])))
-        for j in range(COUNT // FACE):
-            at = slice(j * FACE, (j + 1) * FACE)
-            new = cur[at] + halves(dot(pick_t[at], extg[...]))
-            cur[at] = new
-            ext[at] = split(new)
+        far_part[...] = scatter_side(1)
+
+        @pl.when(k < DEG)
+        def _():
+            @pl.when(k == 0)
+            def _():
+                send_back(1, far_part[...])
+
+            @pl.when(k > 0)
+            def _():
+                take_face(1)
+                send_back(1, far_part[...] + far_far())
+                gather_side(1)
+                apply_cells()
+
+            send_back(0, scatter_side(0))
+            for j, (first, last) in enumerate(CHUNK_BLOCKS):
+                at = slice(j * FACE, (j + 1) * FACE)
+                lanes = slice(CHUNK_AT[j] * ROWS, (CHUNK_AT[j] + last - first) * ROWS)
+                added = halves(dot(t_own[:, lanes], loc[first * ROWS : last * ROWS]))
+                now = cur[at]
+                new = alpha * (added + (pot[at] - centre) * now) - beta * prev[at]
+                prev[at] = now
+                cur[at] = new
+                ext[at] = split(new)
+            face_part[...] = halves(dot(pick[...], ext[...]))
+
+            @pl.when(k == 0)
+            def _():
+                build_far()
+
+            take_back(0, alpha)
+            take_back(1, alpha)
+            send_faces(face_part[...] + halves(dot(cross[...], extr[...])))
+            for j in range(COUNT // FACE):
+                at = slice(j * FACE, (j + 1) * FACE)
+                new = cur[at] + halves(dot(pick_t[at], extr[...]))
+                cur[at] = new
+                ext[at] = split(new)
+
         return carry
 
-    lax.fori_loop(0, DEG, step, 0)
-
     share = 1.0 / (total * COUNT)
-    corr_sum.start_first(quarters(dot(ext[...], ext[...], ((0,), (0,)))) * share)
-    gather_owned()
-    take_faces()
+    lax.fori_loop(0, DEG + 1, step, 0)
+
     corr_sum.start_second()
-    gather_ghosts()
-    apply_cells()
+    gram_acc[...] = jnp.zeros((2 * NS, 2 * NS), F32)
+
+    def gram_block(b, carry):
+        rows = loc[pl.ds(pl.multiple_of(b * ROWS, NS), ROWS)]
+        at = pl.ds(pl.multiple_of(b * FACE, FACE), FACE)
+        gram_acc[...] += dot(gath[b], rows, ((0,), (0,))) + dot(
+            ext[at], split(pot[at] * cur[at]), ((0,), (0,))
+        )
+        return carry
+
+    lax.fori_loop(0, BLOCKS, gram_block, 0)
+    take_face(1)
+    mixed = quarters(dot(extg[FACE:], split(far_part[...] + 0.5 * far_far()), ((0,), (0,))))
+    gram_sum.start_first((quarters(gram_acc[...]) + (mixed + mixed.T)) * share)
     corr_sum.start_third()
-    gram = jnp.zeros((2 * NS, 2 * NS), F32)
-    for b in range(BLOCKS):
-        gram = gram + dot(gath[b], loc[b * ROWS : (b + 1) * ROWS], ((0,), (0,)))
-    for j in range(COUNT // FACE):
-        at = slice(j * FACE, (j + 1) * FACE)
-        gram = gram + dot(ext[at], split(pot[at] * cur[at]), ((0,), (0,)))
-    gram_sum.start_first(quarters(gram) * share)
+    gram_sum.start_second()
     left[...] = corr_sum.finish()
     right[...] = jnp.where(
         lax.broadcasted_iota(jnp.int32, (NS, NS), 0) == lax.broadcasted_iota(jnp.int32, (NS, NS), 1),
         1.0,
         0.0,
     ).astype(F32)
-    for p in range(6):
-        factor_panel(p, left, right)
-    gram_sum.start_second()
-    for p in range(6, NS // 8):
-        factor_panel(p, left, right)
+    def panel(p, carry):
+        factor_panel(p, left, right, inverse)
+        return carry
+
+    lax.fori_loop(0, NS // 16, panel, 0)
     gram_sum.start_third()
-    inv = right[...]
+    lax.fori_loop(NS // 16, NS // 8, panel, 0)
+    inv = inverse[...]
     hi = inv.astype(BF16)
     low = (inv - hi.astype(F32)).astype(BF16)
     wide = jnp.concatenate([hi, hi], axis=1)
@@ -415,10 +517,10 @@
     q = lax.rem(grp, 4)
     jump = 8 * rows_grid
     mine = jnp.concatenate(
-        [right[pl.ds(pl.multiple_of(jump * t + 8 * r, 8), 8)] for t in range(NS // jump)], axis=0
+        [inverse[pl.ds(pl.multiple_of(jump * t + 8 * r, 8), 8)] for t in range(NS // jump)], axis=0
     )
     other = jnp.concatenate(
-        [right[pl.ds(pl.multiple_of(32 * t + 8 * q, 8), 8)] for t in range(NS // 32)], axis=0
+        [inverse[pl.ds(pl.multiple_of(32 * t + 8 * q, 8), 8)] for t in range(NS // 32)], axis=0
     )
     mine = jnp.dot(mine, hgram, precision=high, preferred_element_type=F32)
     tile_ref[...] = lax.dot_general(
@@ -465,6 +567,8 @@
             pltpu.VMEM((BLOCKS * ROWS, 2 * NS), BF16),
             pltpu.VMEM((COUNT, 2 * NS), BF16),
             pltpu.VMEM((GHOST, 2 * NS), BF16),
+            pltpu.VMEM((GHOST, 2 * NS), BF16),
+            pltpu.VMEM((2, FACE, FACE), BF16),
             field,
             field,
             field,
@@ -476,8 +580,13 @@
             faces,
             pltpu.VMEM((NS, NS), F32),
             pltpu.VMEM((NS, NS), F32),
-            dma((4,)),
-            dma((4,)),
+            pltpu.VMEM((NS, NS), F32),
+            pltpu.VMEM((BLOCKS, ROWS, NS), jnp.int32),
+            pltpu.VMEM((BLOCKS, ROWS), jnp.int32),
+            pltpu.VMEM((FACE, NS), F32),
+            pltpu.VMEM((2 * NS, 2 * NS), F32),
+            dma((2, 2)),
+            dma((2, 2)),
             *one_sum,
             *one_sum,
         ],
@@ -498,15 +607,6 @@
     filter_cut,
     spectrum_top,
 ):
-    cells = cell_scale.shape[0]
-    start = jnp.minimum(jnp.arange(cells, dtype=jnp.int32) // 32, 6) * FACE
-    column = jnp.where(
-        connect < FACE,
-        connect + WIN,
-        jnp.where(connect >= FACE + COUNT, connect - FACE - COUNT + WIN + FACE, connect - FACE - start),
-    )
-    column = jnp.pad(column, ((0, SLOTS - NPC), (0, 0)), constant_values=-1)
-    column = column.reshape(SLOTS, BLOCKS, GROUPS, 8).transpose(1, 2, 0, 3).reshape(BLOCKS, ROWS)
     return whole(
         lax.axis_size("dom"),
         lax.axis_size("grp"),
@@ -516,9 +616,9 @@
             node_count,
             states,
             potential.reshape(COUNT // NS, NS),
-            cell_scale.reshape(cells // NS, NS),
+            cell_scale.reshape(CELLS // NS, NS),
             stiffness,
-            column,
+            connect,
             face_nodes,
         ),
     )

time: 134 us -> 115 us (0.86)
  Pallas kernels: 126 us -> 110 us
  local copies, waits for them, and re-layouts: 4.91 us -> 2.88 us
    pallas_call x1, Pallas kernels: 126 us -> 110 us  [whole(): pl.pallas_call(functools.partial(filter_kernel, n_dom, n_grp), out_shape=...]
    unnamed x5 -> x4, local copies, waits for them, and re-layouts: 3.74 us -> 2.88 us
where the time goes in v3:
time: 115 us
  Pallas kernels  110 us (96%)
  local copies, waits for them, and re-layouts  2.88 us (3%)
  between operations  2.59 us (2%)
    pallas_call x1, Pallas kernels, whole(): pl.pallas_call(functools.partial(filter_kernel, n_dom, n_grp), out_shape=...  110 us
    unnamed x4, local copies, waits for them, and re-layouts  2.88 us

profile of v3, /device:TPU:1, one launch (start us, length us, event | category | flops | bytes accessed | tf_op | source)
XLA Modules:
  0.0 115.2 jit_solution(3745317539214039660)
XLA Ops:
  2.6 109.7 %shard_map.104 = (f32[2048,128]{1,0:T(8,128)}, f32[32,32]{1,0:T(8,128)}) custom-call(f32[1]{0:T(128)S(6)} %copy.14.cut_ref, f32[1]{0:T(128)S(6)} %copy.15.top_ref, s32[1]{0:T(128)S(6)} %copy.13.live_ref, f32[2048,128]{1,0:T(8,128)} %states_ref.1, f32[16,128]{1,0:T(8,128)} %bitcast.2, f32[2,128]{1,0:T(2,128)} %bitcast.3, f32[27,27]{1,0:T(8,128)} %kmat_ref.1, ...), custom_call_target="tpu_custom_call" | custom-call | tf_op jit(solution)/shard_map/pallas_call | solution.py:549
  112.3 0.0 copy-start
  112.3 2.3 %copy.16 = f32[2048,128]{1,0:T(8,128)} copy(f32[2048,128]{1,0:T(8,128)} %get-tuple-element.4) | data formatting | bytes 2097152
  114.5 0.0 copy-done
  114.5 0.6 copy.17
Async XLA Ops:
  112.3 2.3 %copy-start = (f32[32,32]{1,0:T(8,128)S(1)}, f32[32,32]{1,0:T(8,128)}, u32[]{:S(2)}) copy-start(f32[32,32]{1,0:T(8,128)} %get-tuple-element.5) | copy-start | bytes 12292

commit v4 on v3

--- a/solution.py
+++ b/solution.py
@@ -52,44 +52,60 @@
 
 class Sum:
     def __init__(self, n_dom, n_grp, dom, grp, refs):
-        self.src, self.slots, self.part, self.doms, self.out, self.sems1, self.sems2, self.sems3 = refs
-        self.n_dom, self.n_grp, self.dom, self.grp = n_dom, n_grp, dom, grp
-
-    def grp_copy(self, s, src, dst, sems):
+        self.src, self.slots, self.part, self.sums, self.out, self.sems1, self.sems2, self.sems3 = refs
+        self.n_in = n_grp // 2
+        self.n_out = 2 * n_dom
+        self.inner = lax.rem(grp, self.n_in)
+        self.outer = dom * 2 + grp // self.n_in
+
+    def device(self, outer, inner):
+        return (outer // 2, lax.rem(outer, 2) * self.n_in + inner)
+
+    def in_partner(self, s):
+        return lax.rem(self.inner + s, self.n_in)
+
+    def partners(self):
+        found = [self.device(self.outer, self.in_partner(s)) for s in range(1, self.n_in)]
+        return found + [
+            self.device(lax.rem(self.outer + s, self.n_out), self.inner) for s in range(1, self.n_out)
+        ]
+
+    def in_copy(self, s, src, dst, sems):
         return pltpu.make_async_remote_copy(
             src_ref=src, dst_ref=dst, send_sem=sems.at[0, s], recv_sem=sems.at[1, s],
-            device_id=(self.dom, lax.rem(self.grp + s, self.n_grp)), device_id_type=MESH,
+            device_id=self.device(self.outer, self.in_partner(s)), device_id_type=MESH,
         )
 
     def first(self):
         return [
-            self.grp_copy(s, self.src.at[lax.rem(self.grp + s, self.n_grp)], self.slots.at[s], self.sems1)
-            for s in range(1, self.n_grp)
+            self.in_copy(s, self.src.at[self.in_partner(s)], self.slots.at[s], self.sems1)
+            for s in range(1, self.n_in)
         ]
 
     def second(self):
         return [
             pltpu.make_async_remote_copy(
-                src_ref=self.part.at[0], dst_ref=self.doms.at[self.dom],
+                src_ref=self.part.at[0], dst_ref=self.sums.at[self.outer],
                 send_sem=self.sems2.at[0, s], recv_sem=self.sems2.at[1, s],
-                device_id=(lax.rem(self.dom + s, self.n_dom), self.grp), device_id_type=MESH,
+                device_id=self.device(lax.rem(self.outer + s, self.n_out), self.inner),
+                device_id_type=MESH,
             )
-            for s in range(1, self.n_dom)
+            for s in range(1, self.n_out)
         ]
 
     def third(self):
         return [
-            self.grp_copy(s, self.part.at[1], self.out.at[self.grp], self.sems3)
-            for s in range(1, self.n_grp)
+            self.in_copy(s, self.part.at[1], self.out.at[self.inner], self.sems3)
+            for s in range(1, self.n_in)
         ]
 
     def start_first(self, value):
-        piece = NS // self.n_grp
-        for j in range(self.n_grp):
+        piece = NS // self.n_in
+        for j in range(self.n_in):
             self.src[j] = value[j * piece : (j + 1) * piece]
         for copy in self.first():
             copy.start()
-        self.slots[0] = self.src[self.grp]
+        self.slots[0] = self.src[self.inner]
 
     def start_second(self):
         for copy in self.first():
@@ -97,15 +113,15 @@
         self.part[0] = jnp.sum(self.slots[...], axis=0)
         for copy in self.second():
             copy.start()
-        self.doms[self.dom] = self.part[0]
+        self.sums[self.outer] = self.part[0]
 
     def start_third(self):
         for copy in self.second():
             copy.wait()
-        self.part[1] = jnp.sum(self.doms[...], axis=0)
+        self.part[1] = jnp.sum(self.sums[...], axis=0)
         for copy in self.third():
             copy.start()
-        self.out[self.grp] = self.part[1]
+        self.out[self.inner] = self.part[1]
 
     def finish(self):
         for copy in self.third():
@@ -199,6 +215,7 @@
     gram_acc,
     face_sems,
     back_sems,
+    states_sem,
     *sums,
 ):
     dom = lax.axis_index("dom")
@@ -213,13 +230,14 @@
     ids = [(at // n_grp, lax.rem(at, n_grp)) for at in (near_at, far_at)]
     edge = jnp.logical_or(me == 0, me == total - 1)
     partners = list(ids)
-    partners += [(dom, lax.rem(grp + s, n_grp)) for s in range(1, n_grp)]
-    partners += [(lax.rem(dom + s, n_dom), grp) for s in range(1, n_dom)]
+    corr_sum = Sum(n_dom, n_grp, dom, grp, sums[: len(sums) // 2])
+    gram_sum = Sum(n_dom, n_grp, dom, grp, sums[len(sums) // 2 :])
+    partners += corr_sum.partners()
+    states_copy = pltpu.make_async_copy(states_ref, cur, states_sem)
+    states_copy.start()
     barrier = pltpu.get_barrier_semaphore()
     for device in partners:
         pl.semaphore_signal(barrier, inc=1, device_id=device, device_id_type=MESH)
-    corr_sum = Sum(n_dom, n_grp, dom, grp, sums[: len(sums) // 2])
-    gram_sum = Sum(n_dom, n_grp, dom, grp, sums[len(sums) // 2 :])
 
     def swap(side, send, recv, sems):
         return pltpu.make_async_remote_copy(
@@ -264,7 +282,7 @@
         start = pl.multiple_of(i * NS, NS)
         at = pl.ds(start, NS)
         node = lax.broadcasted_iota(jnp.int32, (NS, NS), 0) + start
-        value = jnp.where(node < live, states_ref[at], 0.0)
+        value = jnp.where(node < live, cur[at], 0.0)
         cur[at] = value
         prev[at] = jnp.zeros((NS, NS), F32)
         ext[at] = split(value)
@@ -272,6 +290,7 @@
         pick[:, at] = jnp.where(wants == lane, 1.0, 0.0).astype(BF16)
         return carry
 
+    states_copy.wait()
     lax.fori_loop(0, COUNT // NS, first_field, 0)
     face_part[...] = halves(dot(pick[...], ext[...]))
 
@@ -329,7 +348,10 @@
         return carry
 
     lax.fori_loop(0, COUNT // NS, build_pick, 0)
-    cross[...] = dot(pick[...], pick_t[...]).astype(BF16)
+    for side in range(2):
+        row = jnp.broadcast_to(faces[side], (2 * FACE, FACE))
+        want = jnp.concatenate([wants, wants], axis=1)
+        cross[:, side * FACE : (side + 1) * FACE] = jnp.where(want == row, 1.0, 0.0).astype(BF16)
     spread = (
         lax.broadcasted_iota(jnp.int32, (GROWS, NPC), 0) // 8
         == lax.broadcasted_iota(jnp.int32, (GROWS, NPC), 1)
@@ -474,15 +496,18 @@
     corr_sum.start_second()
     gram_acc[...] = jnp.zeros((2 * NS, 2 * NS), F32)
 
-    def gram_block(b, carry):
-        rows = loc[pl.ds(pl.multiple_of(b * ROWS, NS), ROWS)]
-        at = pl.ds(pl.multiple_of(b * FACE, FACE), FACE)
-        gram_acc[...] += dot(gath[b], rows, ((0,), (0,))) + dot(
-            ext[at], split(pot[at] * cur[at]), ((0,), (0,))
-        )
+    def gram_blocks(h, carry):
+        part = gram_acc[...]
+        for t in range(BLOCKS // 2):
+            b = h * (BLOCKS // 2) + t
+            rows = loc[pl.ds(pl.multiple_of(b * ROWS, NS), ROWS)]
+            at = pl.ds(pl.multiple_of(b * FACE, FACE), FACE)
+            part = part + dot(gath[b], rows, ((0,), (0,)))
+            part = part + dot(ext[at], split(pot[at] * cur[at]), ((0,), (0,)))
+        gram_acc[...] = part
         return carry
 
-    lax.fori_loop(0, BLOCKS, gram_block, 0)
+    lax.fori_loop(0, 2, gram_blocks, 0)
     take_face(1)
     mixed = quarters(dot(extg[FACE:], split(far_part[...] + 0.5 * far_far()), ((0,), (0,))))
     gram_sum.start_first((quarters(gram_acc[...]) + (mixed + mixed.T)) * share)
@@ -529,20 +554,21 @@
 
 
 def whole(n_dom, n_grp, operands):
-    piece = NS // n_grp
+    n_in, n_out = n_grp // 2, 2 * n_dom
+    piece = NS // n_in
     rows_grid = n_grp // 4
     vmem = pl.BlockSpec(memory_space=pltpu.VMEM)
     smem = pl.BlockSpec(memory_space=pltpu.SMEM)
     dma = pltpu.SemaphoreType.DMA
     one_sum = [
-        pltpu.VMEM((n_grp, piece, NS), F32),
-        pltpu.VMEM((n_grp, piece, NS), F32),
+        pltpu.VMEM((n_in, piece, NS), F32),
+        pltpu.VMEM((n_in, piece, NS), F32),
         pltpu.VMEM((2, piece, NS), F32),
-        pltpu.VMEM((n_dom, piece, NS), F32),
-        pltpu.VMEM((n_grp, piece, NS), F32),
-        dma((2, n_grp)),
-        dma((2, n_dom)),
-        dma((2, n_grp)),
+        pltpu.VMEM((n_out, piece, NS), F32),
+        pltpu.VMEM((n_in, piece, NS), F32),
+        dma((2, n_in)),
+        dma((2, n_out)),
+        dma((2, n_in)),
     ]
     faces = pltpu.VMEM((2, FACE, NS), F32)
     field = pltpu.VMEM((COUNT, NS), F32)
@@ -552,7 +578,7 @@
             jax.ShapeDtypeStruct((COUNT, NS), F32),
             jax.ShapeDtypeStruct((NS // rows_grid, NS // 4), F32),
         ),
-        in_specs=[smem] * 3 + [vmem] * 6,
+        in_specs=[smem] * 3 + [pl.BlockSpec(memory_space=pl.ANY)] + [vmem] * 5,
         out_specs=(vmem, vmem),
         scratch_shapes=[
             pltpu.VMEM((BLOCKS, ROWS, WIN), BF16),
@@ -587,6 +613,7 @@
             pltpu.VMEM((2 * NS, 2 * NS), F32),
             dma((2, 2)),
             dma((2, 2)),
+            dma,
             *one_sum,
             *one_sum,
         ],

time: 115 us -> 113 us (0.983)
  Pallas kernels: 110 us -> 108 us
    pallas_call x1, Pallas kernels: 110 us -> 108 us  [whole(): pl.pallas_call(functools.partial(filter_kernel, n_dom, n_grp), out_shape=...]
where the time goes in v4:
time: 113 us
  Pallas kernels  108 us (96%)
  local copies, waits for them, and re-layouts  2.88 us (3%)
  between operations  2.59 us (2%)
    pallas_call x1, Pallas kernels, whole(): pl.pallas_call(functools.partial(filter_kernel, n_dom, n_grp), out_shape=...  108 us
    unnamed x4, local copies, waits for them, and re-layouts  2.88 us

profile of v4, /device:TPU:1, one launch (start us, length us, event | category | flops | bytes accessed | tf_op | source)
XLA Modules:
  0.0 113.2 jit_solution(12008682372905720964)
XLA Ops:
  2.6 107.8 %shard_map.104 = (f32[2048,128]{1,0:T(8,128)}, f32[32,32]{1,0:T(8,128)}) custom-call(f32[1]{0:T(128)S(6)} %copy.14.cut_ref, f32[1]{0:T(128)S(6)} %copy.15.top_ref, s32[1]{0:T(128)S(6)} %copy.13.live_ref, f32[2048,128]{1,0:T(8,128)} %states_ref.1, f32[16,128]{1,0:T(8,128)} %bitcast.2, f32[2,128]{1,0:T(2,128)} %bitcast.3, f32[27,27]{1,0:T(8,128)} %kmat_ref.1, ...), custom_call_target="tpu_custom_call" | custom-call | tf_op jit(solution)/shard_map/pallas_call | solution.py:575
  110.3 0.0 copy-start
  110.3 2.3 %copy.16 = f32[2048,128]{1,0:T(8,128)} copy(f32[2048,128]{1,0:T(8,128)} %get-tuple-element.4) | data formatting | bytes 2097152
  112.6 0.0 copy-done
  112.6 0.6 copy.17
Async XLA Ops:
  110.3 2.3 %copy-start = (f32[32,32]{1,0:T(8,128)S(1)}, f32[32,32]{1,0:T(8,128)}, u32[]{:S(2)}) copy-start(f32[32,32]{1,0:T(8,128)} %get-tuple-element.5) | copy-start | bytes 12292

commit v5 on v4

--- a/solution.py
+++ b/solution.py
@@ -127,6 +127,18 @@
         for copy in self.third():
             copy.wait()
         return self.out[...].reshape(NS, NS)
+
+
+def dot_split(a, b, dim):
+    a_hi = a.astype(BF16)
+    a_lo = (a - a_hi.astype(F32)).astype(BF16)
+    b_hi = b.astype(BF16)
+    b_lo = (b - b_hi.astype(F32)).astype(BF16)
+    return dot(
+        jnp.concatenate([a_hi, a_lo, a_hi], axis=1),
+        jnp.concatenate([b_hi, b_hi, b_lo], axis=dim),
+        ((1,), (dim,)),
+    )
 
 
 def triple(x):
@@ -246,10 +258,9 @@
             device_id=ids[side], device_id_type=MESH,
         )
 
-    def send_faces(values):
-        for side in (1, 0):
-            face_send[side] = values[side * FACE : (side + 1) * FACE]
-            swap(side, face_send, face_recv, face_sems).start()
+    def send_face(side, value):
+        face_send[side] = value
+        swap(side, face_send, face_recv, face_sems).start()
 
     def take_face(side):
         swap(side, face_send, face_recv, face_sems).wait()
@@ -318,7 +329,8 @@
     conn_row[...] = packed.T[:BLOCKS].astype(jnp.int32)
 
     pl.semaphore_wait(barrier, len(partners))
-    send_faces(face_part[...])
+    send_face(1, face_part[FACE:])
+    send_face(0, face_part[:FACE])
 
     def build(b, carry):
         col = conn_col[b]
@@ -448,6 +460,11 @@
             gather_side(1)
 
         apply_cells()
+
+        @pl.when(k == DEG)
+        def _():
+            corr_sum.start_second()
+
         far_part[...] = scatter_side(1)
 
         @pl.when(k < DEG)
@@ -481,7 +498,9 @@
 
             take_back(0, alpha)
             take_back(1, alpha)
-            send_faces(face_part[...] + halves(dot(cross[...], extr[...])))
+            for side in (1, 0):
+                at = slice(side * FACE, (side + 1) * FACE)
+                send_face(side, face_part[at] + halves(dot(cross[at], extr[...])))
             for j in range(COUNT // FACE):
                 at = slice(j * FACE, (j + 1) * FACE)
                 new = cur[at] + halves(dot(pick_t[at], extr[...]))
@@ -493,7 +512,6 @@
     share = 1.0 / (total * COUNT)
     lax.fori_loop(0, DEG + 1, step, 0)
 
-    corr_sum.start_second()
     gram_acc[...] = jnp.zeros((2 * NS, 2 * NS), F32)
 
     def gram_blocks(h, carry):
@@ -523,9 +541,9 @@
         factor_panel(p, left, right, inverse)
         return carry
 
-    lax.fori_loop(0, NS // 16, panel, 0)
+    lax.fori_loop(0, 10, panel, 0)
     gram_sum.start_third()
-    lax.fori_loop(NS // 16, NS // 8, panel, 0)
+    lax.fori_loop(10, NS // 8, panel, 0)
     inv = inverse[...]
     hi = inv.astype(BF16)
     low = (inv - hi.astype(F32)).astype(BF16)
@@ -537,7 +555,6 @@
         ortho_ref[at] = halves(dot(ext[at], weights, ((1,), (1,))))
     hgram = gram_sum.finish()
     rows_grid = n_grp // 4
-    high = lax.Precision.HIGHEST
     r = grp // 4
     q = lax.rem(grp, 4)
     jump = 8 * rows_grid
@@ -547,10 +564,8 @@
     other = jnp.concatenate(
         [inverse[pl.ds(pl.multiple_of(32 * t + 8 * q, 8), 8)] for t in range(NS // 32)], axis=0
     )
-    mine = jnp.dot(mine, hgram, precision=high, preferred_element_type=F32)
-    tile_ref[...] = lax.dot_general(
-        mine, other, (((1,), (1,)), ((), ())), precision=high, preferred_element_type=F32
-    )
+    mine = dot_split(mine, hgram, 0)
+    tile_ref[...] = dot_split(mine, other, 1)
 
 
 def whole(n_dom, n_grp, operands):

time: 113 us -> 113 us (level)
  no operation moved by 1% of the time
where the time goes in v5:
time: 113 us
  Pallas kernels  107 us (95%)
  local copies, waits for them, and re-layouts  2.88 us (3%)
  between operations  2.59 us (2%)
    pallas_call x1, Pallas kernels, whole(): pl.pallas_call(functools.partial(filter_kernel, n_dom, n_grp), out_shape=...  107 us
    unnamed x4, local copies, waits for them, and re-layouts  2.88 us

profile of v5, /device:TPU:1, one launch (start us, length us, event | category | flops | bytes accessed | tf_op | source)
XLA Modules:
  0.0 112.7 jit_solution(9369145258216693136)
XLA Ops:
  2.6 107.2 %shard_map.104 = (f32[2048,128]{1,0:T(8,128)}, f32[32,32]{1,0:T(8,128)}) custom-call(f32[1]{0:T(128)S(6)} %copy.14.cut_ref, f32[1]{0:T(128)S(6)} %copy.15.top_ref, s32[1]{0:T(128)S(6)} %copy.13.live_ref, f32[2048,128]{1,0:T(8,128)} %states_ref.1, f32[16,128]{1,0:T(8,128)} %bitcast.2, f32[2,128]{1,0:T(2,128)} %bitcast.3, f32[27,27]{1,0:T(8,128)} %kmat_ref.1, ...), custom_call_target="tpu_custom_call" | custom-call | tf_op jit(solution)/shard_map/pallas_call | solution.py:590
  109.8 0.0 copy-start
  109.8 2.3 %copy.16 = f32[2048,128]{1,0:T(8,128)} copy(f32[2048,128]{1,0:T(8,128)} %get-tuple-element.4) | data formatting | bytes 2097152
  112.0 0.0 copy-done
  112.0 0.6 copy.17
Async XLA Ops:
  109.8 2.3 %copy-start = (f32[32,32]{1,0:T(8,128)S(1)}, f32[32,32]{1,0:T(8,128)}, u32[]{:S(2)}) copy-start(f32[32,32]{1,0:T(8,128)} %get-tuple-element.5) | copy-start | bytes 12292

commit v6 on v5

--- a/solution.py
+++ b/solution.py
@@ -423,8 +423,8 @@
 
     def build_far():
         def far_block(h, carry):
-            for t in range(2):
-                b = 2 * h + t
+            for t in range(BLOCKS // 2):
+                b = h * (BLOCKS // 2) + t
                 for i in range(GROUPS):
                     part = g_gho[b, i * GROWS : (i + 1) * GROWS, FACE:]
                     out = dot(kk[0], part) + dot(kk[1], part)
@@ -438,7 +438,7 @@
                     ).astype(BF16)
             return carry
 
-        lax.fori_loop(0, BLOCKS // 2, far_block, 0)
+        lax.fori_loop(0, 2, far_block, 0)
         out = dot(t_gho[FACE:], gath[...].reshape(BLOCKS * ROWS, FACE)) + dot(t_gho[FACE:], loc[...])
         a_far[0] = out.astype(BF16)
         a_far[1] = (out - out.astype(BF16).astype(F32)).astype(BF16)

time: 113 us -> 113 us (level)
  no operation moved by 1% of the time
where the time goes in v6:
time: 113 us; the launch traced here: 112 us
  Pallas kernels  107 us (95%)
  local copies, waits for them, and re-layouts  2.88 us (3%)
  between operations  2.59 us (2%)
    pallas_call x1, Pallas kernels, whole(): pl.pallas_call(functools.partial(filter_kernel, n_dom, n_grp), out_shape=...  107 us
    unnamed x4, local copies, waits for them, and re-layouts  2.88 us

profile of v6, /device:TPU:1, one launch (start us, length us, event | category | flops | bytes accessed | tf_op | source)
XLA Modules:
  0.0 112.3 jit_solution(16247077683925063524)
XLA Ops:
  2.6 106.8 %shard_map.104 = (f32[2048,128]{1,0:T(8,128)}, f32[32,32]{1,0:T(8,128)}) custom-call(f32[1]{0:T(128)S(6)} %copy.14.cut_ref, f32[1]{0:T(128)S(6)} %copy.15.top_ref, s32[1]{0:T(128)S(6)} %copy.13.live_ref, f32[2048,128]{1,0:T(8,128)} %states_ref.1, f32[16,128]{1,0:T(8,128)} %bitcast.2, f32[2,128]{1,0:T(2,128)} %bitcast.3, f32[27,27]{1,0:T(8,128)} %kmat_ref.1, ...), custom_call_target="tpu_custom_call" | custom-call | tf_op jit(solution)/shard_map/pallas_call | solution.py:590
  109.4 0.0 copy-start
  109.4 2.3 %copy.16 = f32[2048,128]{1,0:T(8,128)} copy(f32[2048,128]{1,0:T(8,128)} %get-tuple-element.4) | data formatting | bytes 2097152
  111.7 0.0 copy-done
  111.7 0.6 copy.17
Async XLA Ops:
  109.4 2.3 %copy-start = (f32[32,32]{1,0:T(8,128)S(1)}, f32[32,32]{1,0:T(8,128)}, u32[]{:S(2)}) copy-start(f32[32,32]{1,0:T(8,128)} %get-tuple-element.5) | copy-start | bytes 12292
